TPU v7x, 256 devices: a whole 4x4x8 slice. The times are simulated.
256 devices in a mesh: tok: 8 (over z_hi, core), win: 4 (over y), wout: 8 (over z_lo, x).
Axes of the slice: x: 4, y: 4, z: 8 (z_hi: 4, z_lo: 2; z = z_hi * 2 + z_lo), core: 2. Of those that a mesh axis runs over, the one named last changes fastest.
Arguments:
- acts: bfloat16 [1024, 8192], P(('tok', 'wout'), 'win'), may hold values from -6 to 6
- gate_weight: bfloat16 [29568, 8192], P(('tok', 'wout'), 'win'), may hold values from -0.0625 to 0.0625
- up_weight: bfloat16 [29568, 8192], P(('tok', 'wout'), 'win'), may hold values from -0.0625 to 0.0625
- hidden_grad: bfloat16 [1024, 29568], P('wout', 'tok'), may hold values from -2 to 2
Outputs:
- input_grad: bfloat16 [1024, 8192], P(('tok', 'wout'), 'win')
- gate_weight_grad: bfloat16 [29568, 8192], P(('tok', 'wout'), 'win')
- up_weight_grad: bfloat16 [29568, 8192], P(('tok', 'wout'), 'win')
All inputs are finite; a program needn't handle non-finite values.
Results may differ from a plain program's by a relative error of at most 0.0049.
Values may be sent and summed in bfloat16 or wider, within the bound.
No kernel may reach another device: no remote copies, remote signals or barrier semaphores. Data moves between devices by JAX's collectives and lax.ppermute only.
A program may use at most 192 MiB of HBM per device.

v0:
```python
import functools

import jax
import jax.numpy as jnp
import numpy as np
from jax import lax
from jax.experimental import pallas as pl
from jax.experimental.pallas import tpu as pltpu
from jax.sharding import Mesh, PartitionSpec as P

F32 = jnp.float32
BF16 = jnp.bfloat16
NX, NY, ZH, ZL, NC = 4, 4, 4, 2, 2
OWNED = 16
BLOCK = ZL * ZH * OWNED
PART = ZH * OWNED


def cost(microseconds):
    return pl.CostEstimate(flops=int(1.1e9 * microseconds), bytes_accessed=1, transcendentals=0)


VMEM = pl.BlockSpec(memory_space=pltpu.VMEM)
SMEM = pl.BlockSpec(memory_space=pltpu.SMEM)
PARAMS = pltpu.CompilerParams(vmem_limit_bytes=16 * 2**20)


def shift(value, axis, by, size):
    return lax.ppermute(value, axis, [(i, (i + by) % size) for i in range(size)])


def x_shift(value, by):
    return shift(value, "x", by, NX)


def y_shift(value, by):
    return shift(value, "y", by, NY)


def core_swap(value):
    return shift(value, "c", 1, NC)


def exchange(value, axes):
    return lax.all_to_all(value, axes, split_axis=0, concat_axis=0, tiled=True)


def rolled(value, by, axis):
    size = value.shape[axis]
    twice = jnp.concatenate([value, value], axis=axis)
    return lax.dynamic_slice_in_dim(twice, by, size, axis)


def after(value, *others):
    return lax.optimization_barrier((value,) + others)[0]


def offset(x, owner):
    return lax.rem(owner - x + 2 * NX, NX)


def part_of(ref, half):
    return ref[...] if ref.shape[0] == PART else ref[half * PART : (half + 1) * PART]


def forward_kernel(half, at_ref, *refs):
    blocks, weights, tokens, outs, pre = refs[:NX], refs[NX : NX + 4], refs[NX + 4], refs[NX + 5 : -1], refs[-1]
    x, y = at_ref[0], at_ref[1]
    for o, block in enumerate(blocks):
        tokens[o * PART : (o + 1) * PART] = part_of(block, half)
    for side, weight in enumerate(weights):
        value = lax.dot_general(tokens[...], weight[...], (((1,), (1,)), ((), ())), preferred_element_type=F32)
        for o in range(NX):
            pre[o] = value[o * PART : (o + 1) * PART]
        for s, out in enumerate(outs):
            out[side] = pre[offset(x, y + s)].astype(out.dtype)


def forward(at, half, blocks, weights):
    units, width = weights[0].shape
    part = jax.ShapeDtypeStruct((4, PART, units), BF16)
    return pl.pallas_call(
        functools.partial(forward_kernel, half),
        out_shape=(
            jax.ShapeDtypeStruct((NX * PART, width), BF16),
            jax.ShapeDtypeStruct((4, PART, units), F32),
            part,
            part,
            part,
        ),
        in_specs=[SMEM] + [VMEM] * 8,
        out_specs=(VMEM,) * 5,
        scratch_shapes=[pltpu.VMEM((NX, PART, units), F32)],
        compiler_params=PARAMS,
        cost_estimate=cost(0.1),
        name="forward%d" % half,
    )(at, *blocks, *weights)


def gradient_kernel(half, at_ref, own, from1, from2, from3, cot, cot_sibling, out, grad):
    x, c, zl = at_ref[0], at_ref[2], at_ref[3]
    for k, cotangent in enumerate((cot, cot_sibling)):
        for z in range(ZH):
            x_from = lax.rem(x - (z % 2) * NC - c + NX, NX)
            zl_from = lax.rem(zl + z // 2, ZL)
            grad[z * OWNED : (z + 1) * OWNED, :] = cotangent[x_from, zl_from, pl.ds(half * OWNED, OWNED), :]

        def total(side):
            near = own[side] + from1[side].astype(F32)
            return near + (from2[side].astype(F32) + from3[side].astype(F32))

        gate_pre, up_pre = total(2 * k), total(2 * k + 1)
        gate_sig = jax.nn.sigmoid(gate_pre)
        scaled = grad[...].astype(F32) * gate_sig
        out[2 * k] = (scaled * up_pre * (1.0 + gate_pre * (1.0 - gate_sig))).astype(BF16)
        out[2 * k + 1] = (scaled * gate_pre).astype(BF16)


def gradient(at, half, own, received, cot, cot_sibling):
    return pl.pallas_call(
        functools.partial(gradient_kernel, half),
        out_shape=jax.ShapeDtypeStruct(own.shape, BF16),
        in_specs=[SMEM] + [VMEM] * 6,
        out_specs=VMEM,
        scratch_shapes=[pltpu.VMEM(own.shape[1:], BF16)],
        compiler_params=PARAMS,
        cost_estimate=cost(0.1 + 6 * half),
        name="gradient%d" % half,
    )(at, own, *received, cot, cot_sibling)


def backward_kernel(tile, at_ref, own, from1, from2, from3, *refs):
    weights, fulls, outs = refs[:4], refs[4:6], refs[6:]
    x, y = at_ref[0], at_ref[1]
    for side in range(4):
        for s, ref in enumerate((own, from1, from2, from3)):
            fulls[side // 2][side % 2, offset(x, y - s)] = ref[side]
    rows = [fulls[side // 2][side % 2].reshape(NX * PART, own.shape[2]) for side in range(4)]
    for col in range(0, outs[0].shape[1], tile):
        total = None
        for side, weight in enumerate(weights):
            term = jnp.dot(rows[side], weight[:, col : col + tile], preferred_element_type=F32)
            total = term if total is None else total + term
        for o, out in enumerate(outs):
            out[:, col : col + tile] = total[o * PART : (o + 1) * PART].astype(out.dtype)


def backward(at, half, pieces, weights):
    units, width = weights[0].shape
    part = jax.ShapeDtypeStruct((PART, width), BF16)
    full = jax.ShapeDtypeStruct((2, NX, PART, units), BF16)
    return pl.pallas_call(
        functools.partial(backward_kernel, min(512, width)),
        out_shape=(
            full,
            full,
            jax.ShapeDtypeStruct((PART, width), F32),
            part,
            part,
            part,
        ),
        in_specs=[SMEM] + [VMEM] * 8,
        out_specs=(VMEM,) * 6,
        compiler_params=PARAMS,
        cost_estimate=cost(5),
        name="backward%d" % half,
    )(at, *pieces, *weights)


def weights_kernel(side, tile, *refs):
    n = len(refs) // 2
    tokens, fulls, out = refs[:n], refs[n : 2 * n], refs[-1]
    rows = jnp.concatenate([f[side].reshape(NX * PART, out.shape[0]) for f in fulls], axis=0)
    for col in range(0, out.shape[1], tile):
        total = lax.dot_general(
            rows,
            jnp.concatenate([r[:, col : col + tile] for r in tokens], axis=0),
            (((0,), (0,)), ((), ())),
            preferred_element_type=F32,
        )
        out[:, col : col + tile] = total.astype(BF16)


def weight_grad(tokens, fulls, side):
    width = tokens[0].shape[1]
    return pl.pallas_call(
        functools.partial(weights_kernel, side, min(512, width)),
        out_shape=jax.ShapeDtypeStruct((fulls[0].shape[3], width), BF16),
        in_specs=[VMEM] * (2 * len(tokens)),
        out_specs=VMEM,
        compiler_params=PARAMS,
        cost_estimate=cost(5),
        name="weight_grad%d" % side,
    )(*tokens, *fulls)


def halves_kernel(a, b, a_out, b_out):
    a_out[...] = a[: a_out.shape[0]]
    b_out[...] = b[b_out.shape[0] :]


def halves(a, b):
    rows, width = a.shape
    out = jax.ShapeDtypeStruct((rows // 2, width), a.dtype)
    return pl.pallas_call(
        halves_kernel,
        out_shape=(out, out),
        in_specs=[VMEM] * 2,
        out_specs=(VMEM, VMEM),
        compiler_params=PARAMS,
        cost_estimate=cost(0.1),
        name="halves",
    )(a, b)


def local(acts, gate_weight, up_weight, hidden_grad):
    rows, width = acts.shape
    units = gate_weight.shape[0]
    x, y, c, zl = lax.axis_index("x"), lax.axis_index("y"), lax.axis_index("c"), lax.axis_index("zl")
    at = jnp.stack([x, y, c, zl]).astype(jnp.int32)

    weights = [gate_weight, up_weight, core_swap(gate_weight), core_swap(up_weight)]

    cot = hidden_grad.reshape(ZL, NX, OWNED, ZL, NX, units)
    cot = lax.dynamic_index_in_dim(cot, y, 1, keepdims=False).reshape(ZL * OWNED, ZL, NX, units)
    cot = rolled(rolled(cot.transpose(1, 2, 0, 3), zl, 0), x, 1)

    mine = exchange(jnp.broadcast_to(acts[None], (ZL * ZH, rows, width)), ("zl", "zh")).reshape(BLOCK, width)
    mine, cot, *weights = lax.optimization_barrier((mine, cot, *weights))
    right = x_shift(mine, -1)
    left = x_shift(mine, 1)

    passed = shift(cot[1], "zl", 1, ZL)
    cot = [jnp.stack([cot[0, s], passed[s]]) for s in range(NX)]
    cot = jnp.stack([cot[0]] + [x_shift(cot[s], s) for s in range(1, NX)])

    right_half, left_half = halves(right, left)
    far = lax.optimization_barrier((x_shift(right_half, -1), x_shift(left_half, 1)))
    chunks = [[mine, right, f, left] for f in far]

    cot_sibling = core_swap(cot)
    tokens0, own0, *sent0 = forward(after(at, cot_sibling), 0, chunks[0], weights)
    got0 = [y_shift(t, s) for s, t in enumerate(sent0, 1)]
    tokens1, own1, *sent1 = forward(after(at, own0), 1, chunks[1], weights)
    got0, sent1 = lax.optimization_barrier((got0, sent1))
    got1 = [y_shift(t, s) for s, t in enumerate(sent1, 1)]
    grad0 = gradient(at, 0, own0, got0, cot, cot_sibling)
    pieces0 = [grad0] + [y_shift(grad0, s) for s in (1, 2, 3)]
    grad1 = gradient(after(at, grad0), 1, own1, got1, cot, cot_sibling)
    pieces1 = [grad1] + [y_shift(grad1, s) for s in (1, 2, 3)]

    full0, passed0, kept0, *parts0 = backward(after(at, grad1), 0, pieces0, weights)
    sums0 = [x_shift(part, o) for o, part in enumerate(parts0, 1)]
    full1, passed1, kept1, *parts1 = backward(after(at, kept0), 1, pieces1, weights)
    parts1, sums0 = lax.optimization_barrier((parts1, sums0))
    sums1 = [x_shift(part, o) for o, part in enumerate(parts1, 1)]

    totals = []
    for kept, sums in ((kept0, sums0), (kept1, sums1)):
        for part in sums:
            kept = kept + part.astype(F32)
        totals.append(kept.astype(BF16))
    total = jnp.concatenate(totals, axis=0)
    got = exchange(total.reshape(ZL * ZH, rows, width), ("zl", "zh"))
    tokens0, tokens1, kept1 = lax.optimization_barrier((tokens0, tokens1, kept1))
    tokens = [tokens0, tokens1, core_swap(tokens0), core_swap(tokens1)]
    fulls = [full0, full1, core_swap(passed0), core_swap(passed1)]
    gate_weight_grad, up_weight_grad = [weight_grad(tokens, fulls, side) for side in (0, 1)]
    got, gate_weight_grad, up_weight_grad = lax.optimization_barrier((got, gate_weight_grad, up_weight_grad))
    input_grad = got.astype(F32).sum(axis=0).astype(BF16)
    return input_grad, gate_weight_grad, up_weight_grad


def solution(mesh):
    fine = Mesh(np.asarray(mesh.devices).reshape(ZH, NC, NY, ZL, NX), ("zh", "c", "y", "zl", "x"))
    rows = ("zh", "c", "zl", "x")
    in_specs = (P(rows, "y"), P(rows, "y"), P(rows, "y"), P(("zl", "x"), ("zh", "c")))
    out_specs = (P(rows, "y"), P(rows, "y"), P(rows, "y"))
    return jax.shard_map(local, mesh=fine, in_specs=in_specs, out_specs=out_specs, check_vma=False)
```

profile of v0, /device:TPU:32, one launch (start us, length us, event | category | flops | bytes accessed | tf_op | source)
XLA Modules:
  0.0 158.5 jit_solution(2349396261220183767)
XLA Ops:
  2.9 8.6 %all-to-all-start = ((bf16[8,16,2048]{2,1,0:T(8,128)(2,1)}), bf16[8,16,2048]{2,1,0:T(8,128)(2,1)S(1)}, u32[]{:S(2)}, u32[]{:S(2)}) async-start(bf16[8,16,2048]{2,1,0:T(8,128)(2,1)} %broadcast_in_dim.2), calls=%async_computation | async-start | bytes 1048576 | tf_op jit(solution)/shard_map/all_to_all | solution.py:45
  12.7 2.3 %reshape.21 = bf16[2,4,16,2,4,462]{5,4,3,2,1,0:T(4,128)(2,1)S(1)} reshape(bf16[128,3696]{1,0:T(8,128)(2,1)S(1)} %copy.8) | data formatting | bytes 1892352 | tf_op jit(solution)/shard_map/reshape | solution.py:224
  16.1 11.6 %all-to-all-done = bf16[8,16,2048]{2,1,0:T(8,128)(2,1)S(1)} async-done(((bf16[8,16,2048]{2,1,0:T(8,128)(2,1)}), bf16[8,16,2048]{2,1,0:T(8,128)(2,1)S(1)}, u32[]{:S(2)}, u32[]{:S(2)}) %all-to-all-start) | async-done | bytes 524320 | tf_op jit(solution)/shard_map/all_to_all | solution.py:45
  29.3 1.7 %collective-permute-start.7 = (bf16[128,2048]{1,0:T(8,128)(2,1)S(1)}, bf16[128,2048]{1,0:T(8,128)(2,1)S(1)}, u32[]{:S(2)}, u32[]{:S(2)}) collective-permute-start(bf16[128,2048]{1,0:T(8,128)(2,1)S(1)} %bitcast.25), channel_id=1, source_target_pairs={{0,3},{1,0},{2,1},{3,2},{4,7},{5,4},{6,5},{7,6},{8,11},{9,8},{10,9... | collective-permute-start | bytes 1572872 | tf_op jit(solution)/shard_map/ppermute | solution.py:29
  32.9 4.1 %collective-permute-done.2 = bf16[4,32,462]{2,1,0:T(8,128)(2,1)S(1)} collective-permute-done((bf16[4,32,462]{2,1,0:T(8,128)(2,1)S(1)}, bf16[4,32,462]{2,1,0:T(8,128)(2,1)S(1)}, u32[]{:S(2)}, u32[]{:S(2)}) %collective-permute-start.2) | collective-permute-done | bytes 118304 | tf_op jit(solution)/shard_map/ppermute | solution.py:29
  37.4 2.8 %collective-permute-start.4 = (bf16[2,32,462]{2,1,0:T(8,128)(2,1)S(1)}, bf16[2,32,462]{2,1,0:T(8,128)(2,1)S(1)}, u32[]{:S(2)}, u32[]{:S(2)}) collective-permute-start(bf16[2,32,462]{2,1,0:T(8,128)(2,1)S(1)} %pad_maximum_fusion.3), channel_id=1, source_target_pairs={{0,2},{1,3},{2,0},{3,1},{4,6},{5,7},{6,4},{7,5},{8,10},{9,11},{10,... | collective-permute-start | bytes 177416 | tf_op jit(solution)/shard_map/ppermute | solution.py:29
  44.1 3.6 %collective-permute-start.9 = (bf16[64,2048]{1,0:T(8,128)(2,1)}, bf16[64,2048]{1,0:T(8,128)(2,1)}, u32[]{:S(2)}, u32[]{:S(2)}) collective-permute-start(bf16[64,2048]{1,0:T(8,128)(2,1)} %get-tuple-element.60), channel_id=1, source_target_pairs={{0,3},{1,0},{2,1},{3,2},{4,7},{5,4},{6,5},{7,6},{8,11},{9,8},{10,9... | collective-permute-start | bytes 786440 | tf_op jit(solution)/shard_map/ppermute | solution.py:29
  48.5 1.8 %collective-permute-done.6.cot_sibling = bf16[4,2,32,462]{3,2,1,0:T(8,128)(2,1)} collective-permute-done((bf16[4,2,32,462]{3,2,1,0:T(8,128)(2,1)}, bf16[4,2,32,462]{3,2,1,0:T(8,128)(2,1)}, u32[]{:S(2)}, u32[]{:S(2)}) %collective-permute-start.6) | collective-permute-done | bytes 236576 | tf_op jit(solution)/shard_map/ppermute | solution.py:29
  51.9 3.7 %collective-permute-done.10.refs_2_ = bf16[64,2048]{1,0:T(8,128)(2,1)} collective-permute-done((bf16[64,2048]{1,0:T(8,128)(2,1)}, bf16[64,2048]{1,0:T(8,128)(2,1)}, u32[]{:S(2)}, u32[]{:S(2)}) %collective-permute-start.10) | collective-permute-done | bytes 262176 | tf_op jit(solution)/shard_map/ppermute | solution.py:29
  57.1 4.9 %forward0.1 = (bf16[256,2048]{1,0:T(8,128)(2,1)}, f32[4,64,462]{2,1,0:T(8,128)S(1)}, bf16[4,64,462]{2,1,0:T(8,128)(2,1)S(1)}, bf16[4,64,462]{2,1,0:T(8,128)(2,1)S(1)}, bf16[4,64,462]{2,1,0:T(8,128)(2,1)S(1)}) custom-call(s32[4]{0:T(128)S(1)} %pad_add_fusion.at_ref, bf16[128,2048]{1,0:T(8,128)(2,1)S(1)} %bitcast.26, ...), custom_call_target="tpu_custom_call" | custom-call | flops 110000000 | bytes 1 | tf_op jit(solution)/shard_map/forward0/pallas_call | solution.py:82
  63.7 2.9 %collective-permute-start.12 = (bf16[4,64,462]{2,1,0:T(8,128)(2,1)S(1)}, bf16[4,64,462]{2,1,0:T(8,128)(2,1)S(1)}, u32[]{:S(2)}, u32[]{:S(2)}) collective-permute-start(bf16[4,64,462]{2,1,0:T(8,128)(2,1)S(1)} %get-tuple-element.69), channel_id=1, source_target_pairs={{0,16},{8,24},{16,0},{24,8},{1,17},{9,25},{17,1},{25,9},{2,18},{10... | collective-permute-start | bytes 709640 | tf_op jit(solution)/shard_map/ppermute | solution.py:29
  67.9 4.8 %forward1.1 = (bf16[256,2048]{1,0:T(8,128)(2,1)}, f32[4,64,462]{2,1,0:T(8,128)S(1)}, bf16[4,64,462]{2,1,0:T(8,128)(2,1)S(1)}, bf16[4,64,462]{2,1,0:T(8,128)(2,1)S(1)}, bf16[4,64,462]{2,1,0:T(8,128)(2,1)S(1)}) custom-call(s32[4]{0:T(128)S(1)} %pad_add_fusion.at_ref, bf16[128,2048]{1,0:T(8,128)(2,1)S(1)} %bitcast.27, ...), custom_call_target="tpu_custom_call" | custom-call | flops 110000000 | bytes 1 | tf_op jit(solution)/shard_map/forward1/pallas_call | solution.py:82
  72.7 3.0 %collective-permute-done.12.from2 = bf16[4,64,462]{2,1,0:T(8,128)(2,1)S(1)} collective-permute-done((bf16[4,64,462]{2,1,0:T(8,128)(2,1)S(1)}, bf16[4,64,462]{2,1,0:T(8,128)(2,1)S(1)}, u32[]{:S(2)}, u32[]{:S(2)}) %collective-permute-start.12) | collective-permute-done | bytes 236576 | tf_op jit(solution)/shard_map/ppermute | solution.py:29
  75.7 4.1 %collective-permute-start.14 = (bf16[4,64,462]{2,1,0:T(8,128)(2,1)S(1)}, bf16[4,64,462]{2,1,0:T(8,128)(2,1)S(1)}, u32[]{:S(2)}, u32[]{:S(2)}) collective-permute-start(bf16[4,64,462]{2,1,0:T(8,128)(2,1)S(1)} %get-tuple-element.81), channel_id=1, source_target_pairs={{0,8},{8,16},{16,24},{24,0},{1,9},{9,17},{17,25},{25,1},{2,10},{10... | collective-permute-start | bytes 709640 | tf_op jit(solution)/shard_map/ppermute | solution.py:29
  80.8 1.7 %collective-permute-start.16 = (bf16[4,64,462]{2,1,0:T(8,128)(2,1)S(1)}, bf16[4,64,462]{2,1,0:T(8,128)(2,1)S(1)}, u32[]{:S(2)}, u32[]{:S(2)}) collective-permute-start(bf16[4,64,462]{2,1,0:T(8,128)(2,1)S(1)} %get-tuple-element.83), channel_id=1, source_target_pairs={{0,24},{8,0},{16,8},{24,16},{1,25},{9,1},{17,9},{25,17},{2,26},{10... | collective-permute-start | bytes 709640 | tf_op jit(solution)/shard_map/ppermute | solution.py:29
  86.3 1.8 %collective-permute-done.14.from1 = bf16[4,64,462]{2,1,0:T(8,128)(2,1)S(1)} collective-permute-done((bf16[4,64,462]{2,1,0:T(8,128)(2,1)S(1)}, bf16[4,64,462]{2,1,0:T(8,128)(2,1)S(1)}, u32[]{:S(2)}, u32[]{:S(2)}) %collective-permute-start.14) | collective-permute-done | bytes 236576 | tf_op jit(solution)/shard_map/ppermute | solution.py:29
  88.1 5.6 %collective-permute-done.15.from2 = bf16[4,64,462]{2,1,0:T(8,128)(2,1)S(1)} collective-permute-done((bf16[4,64,462]{2,1,0:T(8,128)(2,1)S(1)}, bf16[4,64,462]{2,1,0:T(8,128)(2,1)S(1)}, u32[]{:S(2)}, u32[]{:S(2)}) %collective-permute-start.15) | collective-permute-done | bytes 236576 | tf_op jit(solution)/shard_map/ppermute | solution.py:29
  95.0 2.1 %collective-permute-start.22 = (bf16[4,64,462]{2,1,0:T(8,128)(2,1)S(1)}, bf16[4,64,462]{2,1,0:T(8,128)(2,1)S(1)}, u32[]{:S(2)}, u32[]{:S(2)}) collective-permute-start(bf16[4,64,462]{2,1,0:T(8,128)(2,1)S(1)} %gradient1.1.own), channel_id=1, source_target_pairs={{0,24},{8,0},{16,8},{24,16},{1,25},{9,1},{17,9},{25,17},{2,26},{10... | collective-permute-start | bytes 709640 | tf_op jit(solution)/shard_map/ppermute | solution.py:29
  97.1 2.5 %collective-permute-start.21 = (bf16[4,64,462]{2,1,0:T(8,128)(2,1)S(1)}, bf16[4,64,462]{2,1,0:T(8,128)(2,1)S(1)}, u32[]{:S(2)}, u32[]{:S(2)}) collective-permute-start(bf16[4,64,462]{2,1,0:T(8,128)(2,1)S(1)} %gradient1.1.own), channel_id=1, source_target_pairs={{0,16},{8,24},{16,0},{24,8},{1,17},{9,25},{17,1},{25,9},{2,18},{10... | collective-permute-start | bytes 709640 | tf_op jit(solution)/shard_map/ppermute | solution.py:29
  99.6 1.7 %collective-permute-start.20 = (bf16[4,64,462]{2,1,0:T(8,128)(2,1)S(1)}, bf16[4,64,462]{2,1,0:T(8,128)(2,1)S(1)}, u32[]{:S(2)}, u32[]{:S(2)}) collective-permute-start(bf16[4,64,462]{2,1,0:T(8,128)(2,1)S(1)} %gradient1.1.own), channel_id=1, source_target_pairs={{0,8},{8,16},{16,24},{24,0},{1,9},{9,17},{17,25},{25,1},{2,10},{10... | collective-permute-start | bytes 709640 | tf_op jit(solution)/shard_map/ppermute | solution.py:29
  101.8 4.5 %backward0.1 = (bf16[2,4,64,462]{3,2,1,0:T(8,128)(2,1)S(1)}, bf16[2,4,64,462]{3,2,1,0:T(8,128)(2,1)S(1)}, f32[64,2048]{1,0:T(8,128)S(1)}, bf16[64,2048]{1,0:T(8,...) custom-call(s32[4]{0:T(128)S(1)} %pad_add_fusion.at_ref, ...), custom_call_target="tpu_custom_call" | custom-call | flops 5500000256 | bytes 1 | tf_op jit(solution)/shard_map/backward0/pallas_call | solution.py:152
  107.1 5.1 %collective-permute-start.24 = (bf16[64,2048]{1,0:T(8,128)(2,1)S(1)}, bf16[64,2048]{1,0:T(8,128)(2,1)S(1)}, u32[]{:S(2)}, u32[]{:S(2)}) collective-permute-start(bf16[64,2048]{1,0:T(8,128)(2,1)S(1)} %get-tuple-element.91), channel_id=1, source_target_pairs={{0,2},{1,3},{2,0},{3,1},{4,6},{5,7},{6,4},{7,5},{8,10},{9,11},{10,... | collective-permute-start | bytes 786440 | tf_op jit(solution)/shard_map/ppermute | solution.py:29
  112.3 4.5 %backward1.1 = (bf16[2,4,64,462]{3,2,1,0:T(8,128)(2,1)S(1)}, bf16[2,4,64,462]{3,2,1,0:T(8,128)(2,1)S(1)}, f32[64,2048]{1,0:T(8,128)S(1)}, bf16[64,2048]{1,0:T(8,...) custom-call(s32[4]{0:T(128)S(1)} %pad_add_fusion.at_ref, ...), custom_call_target="tpu_custom_call" | custom-call | flops 5500000256 | bytes 1 | tf_op jit(solution)/shard_map/backward1/pallas_call | solution.py:152
  117.9 3.4 %collective-permute-done.24 = bf16[64,2048]{1,0:T(8,128)(2,1)S(1)} collective-permute-done((bf16[64,2048]{1,0:T(8,128)(2,1)S(1)}, bf16[64,2048]{1,0:T(8,128)(2,1)S(1)}, u32[]{:S(2)}, u32[]{:S(2)}) %collective-permute-start.24) | collective-permute-done | bytes 262176 | tf_op jit(solution)/shard_map/ppermute | solution.py:29
  121.3 3.5 %collective-permute-start.27 = (bf16[64,2048]{1,0:T(8,128)(2,1)S(1)}, bf16[64,2048]{1,0:T(8,128)(2,1)S(1)}, u32[]{:S(2)}, u32[]{:S(2)}) collective-permute-start(bf16[64,2048]{1,0:T(8,128)(2,1)S(1)} %get-tuple-element.98), channel_id=1, source_target_pairs={{0,2},{1,3},{2,0},{3,1},{4,6},{5,7},{6,4},{7,5},{8,10},{9,11},{10,... | collective-permute-start | bytes 786440 | tf_op jit(solution)/shard_map/ppermute | solution.py:29
  125.0 5.9 %collective-permute-done.26 = bf16[64,2048]{1,0:T(8,128)(2,1)S(1)} collective-permute-done((bf16[64,2048]{1,0:T(8,128)(2,1)S(1)}, bf16[64,2048]{1,0:T(8,128)(2,1)S(1)}, u32[]{:S(2)}, u32[]{:S(2)}) %collective-permute-start.26) | collective-permute-done | bytes 262176 | tf_op jit(solution)/shard_map/ppermute | solution.py:29
  130.8 4.3 %collective-permute-done.27 = bf16[64,2048]{1,0:T(8,128)(2,1)S(1)} collective-permute-done((bf16[64,2048]{1,0:T(8,128)(2,1)S(1)}, bf16[64,2048]{1,0:T(8,128)(2,1)S(1)}, u32[]{:S(2)}, u32[]{:S(2)}) %collective-permute-start.27) | collective-permute-done | bytes 262176 | tf_op jit(solution)/shard_map/ppermute | solution.py:29
  136.1 4.4 %all-to-all-start.1 = ((bf16[8,16,2048]{2,1,0:T(8,128)(2,1)}), bf16[8,16,2048]{2,1,0:T(8,128)(2,1)}, u32[]{:S(2)}, u32[]{:S(2)}) async-start(bf16[8,16,2048]{2,1,0:T(8,128)(2,1)} %bitcast.28), calls=%async_computation.1 | async-start | bytes 1048576 | tf_op jit(solution)/shard_map/all_to_all | solution.py:45
  142.6 5.2 %weight_grad1.1 = bf16[462,2048]{1,0:T(8,128)(2,1)} custom-call(bf16[256,2048]{1,0:T(8,128)(2,1)} %get-tuple-element.102.refs_0_, bf16[256,2048]{1,0:T(8,128)(2,1)} %get-tuple-element.103.refs_1_, bf16[256,2048]{1,0:T(8,128)(2,1)S(1)} %collective-permute-done.29.refs_2_, bf16[256,2048]{1,0:T(8,128)(2,1)S(1)} %collective-permute-done.30.refs_3_, ...), custom_call_target="tpu_custom_call" | custom-call | flops 5500000256 | bytes 1 | tf_op jit(solution)/shard_map/weight_grad1/pallas_call | solution.py:186
  147.9 5.2 %weight_grad0.1 = bf16[462,2048]{1,0:T(8,128)(2,1)} custom-call(bf16[256,2048]{1,0:T(8,128)(2,1)} %get-tuple-element.102.refs_0_, bf16[256,2048]{1,0:T(8,128)(2,1)} %get-tuple-element.103.refs_1_, bf16[256,2048]{1,0:T(8,128)(2,1)S(1)} %collective-permute-done.29.refs_2_, bf16[256,2048]{1,0:T(8,128)(2,1)S(1)} %collective-permute-done.30.refs_3_, ...), custom_call_target="tpu_custom_call" | custom-call | flops 5500000256 | bytes 1 | tf_op jit(solution)/shard_map/weight_grad0/pallas_call | solution.py:186
  153.1 3.6 %all-to-all-done.1 = bf16[8,16,2048]{2,1,0:T(8,128)(2,1)} async-done(((bf16[8,16,2048]{2,1,0:T(8,128)(2,1)}), bf16[8,16,2048]{2,1,0:T(8,128)(2,1)}, u32[]{:S(2)}, u32[]{:S(2)}) %all-to-all-start.1) | async-done | bytes 524320 | tf_op jit(solution)/shard_map/all_to_all | solution.py:45
  156.8 1.8 %reduce_sum.12 = bf16[16,2048]{1,0:T(8,128)(2,1)} reduce(bf16[8,16,2048]{2,1,0:T(8,128)(2,1)} %all-to-all-done.1, bf16[]{:T(256)} %constant.28.clone.1), dimensions={0}, to_apply=%region_0.1 | reduce | flops 229376 | bytes 589826 | tf_op jit(solution)/shard_map/reduce_sum | solution.py:270
  (83 shorter events, 30.7 us)
Async XLA Ops:
  0.6 27.2 %collective-permute-start = (bf16[462,2048]{1,0:T(8,128)(2,1)}, bf16[462,2048]{1,0:T(8,128)(2,1)}, u32[]{:S(2)}, u32[]{:S(2)}) collective-permute-start(bf16[462,2048]{1,0:T(8,128)(2,1)} %refs_0_.1), channel_id=1, source_target_pairs={{0,32},{32,0},{1,33},{33,1},{2,34},{34,2},{3,35},{35,3},{4,36},{36... | collective-permute-start | bytes 5677064 | tf_op jit(solution)/shard_map/ppermute | solution.py:29
  0.7 27.1 %collective-permute-start.1 = (bf16[462,2048]{1,0:T(8,128)(2,1)}, bf16[462,2048]{1,0:T(8,128)(2,1)}, u32[]{:S(2)}, u32[]{:S(2)}) collective-permute-start(bf16[462,2048]{1,0:T(8,128)(2,1)} %refs_1_.1), channel_id=1, source_target_pairs={{0,32},{32,0},{1,33},{33,1},{2,34},{34,2},{3,35},{35,3},{4,36},{36... | collective-permute-start | bytes 5677064 | tf_op jit(solution)/shard_map/ppermute | solution.py:29
  2.9 24.9 %all-to-all-start = ((bf16[8,16,2048]{2,1,0:T(8,128)(2,1)}), bf16[8,16,2048]{2,1,0:T(8,128)(2,1)S(1)}, u32[]{:S(2)}, u32[]{:S(2)}) async-start(bf16[8,16,2048]{2,1,0:T(8,128)(2,1)} %broadcast_in_dim.2), calls=%async_computation | async-start | bytes 1048576 | tf_op jit(solution)/shard_map/all_to_all | solution.py:45
  27.8 15.1 %collective-permute-start.8 = (bf16[128,2048]{1,0:T(8,128)(2,1)S(1)}, bf16[128,2048]{1,0:T(8,128)(2,1)S(1)}, u32[]{:S(2)}, u32[]{:S(2)}) collective-permute-start(bf16[128,2048]{1,0:T(8,128)(2,1)S(1)} %bitcast.24), channel_id=1, source_target_pairs={{0,1},{1,2},{2,3},{3,0},{4,5},{5,6},{6,7},{7,4},{8,9},{9,10},{10,1... | collective-permute-start | bytes 1572872 | tf_op jit(solution)/shard_map/ppermute | solution.py:29
  29.3 13.9 %collective-permute-start.7 = (bf16[128,2048]{1,0:T(8,128)(2,1)S(1)}, bf16[128,2048]{1,0:T(8,128)(2,1)S(1)}, u32[]{:S(2)}, u32[]{:S(2)}) collective-permute-start(bf16[128,2048]{1,0:T(8,128)(2,1)S(1)} %bitcast.25), channel_id=1, source_target_pairs={{0,3},{1,0},{2,1},{3,2},{4,7},{5,4},{6,5},{7,6},{8,11},{9,8},{10,9... | collective-permute-start | bytes 1572872 | tf_op jit(solution)/shard_map/ppermute | solution.py:29
  37.0 10.6 %collective-permute-start.3 = (bf16[2,32,462]{2,1,0:T(8,128)(2,1)S(1)}, bf16[2,32,462]{2,1,0:T(8,128)(2,1)S(1)}, u32[]{:S(2)}, u32[]{:S(2)}) collective-permute-start(bf16[2,32,462]{2,1,0:T(8,128)(2,1)S(1)} %pad_maximum_fusion.2), channel_id=1, source_target_pairs={{0,1},{1,2},{2,3},{3,0},{4,5},{5,6},{6,7},{7,4},{8,9},{9,10},{10,1... | collective-permute-start | bytes 177416 | tf_op jit(solution)/shard_map/ppermute | solution.py:29
  37.4 10.3 %collective-permute-start.4 = (bf16[2,32,462]{2,1,0:T(8,128)(2,1)S(1)}, bf16[2,32,462]{2,1,0:T(8,128)(2,1)S(1)}, u32[]{:S(2)}, u32[]{:S(2)}) collective-permute-start(bf16[2,32,462]{2,1,0:T(8,128)(2,1)S(1)} %pad_maximum_fusion.3), channel_id=1, source_target_pairs={{0,2},{1,3},{2,0},{3,1},{4,6},{5,7},{6,4},{7,5},{8,10},{9,11},{10,... | collective-permute-start | bytes 177416 | tf_op jit(solution)/shard_map/ppermute | solution.py:29
  40.2 7.4 %collective-permute-start.5 = (bf16[2,32,462]{2,1,0:T(8,128)(2,1)S(1)}, bf16[2,32,462]{2,1,0:T(8,128)(2,1)S(1)}, u32[]{:S(2)}, u32[]{:S(2)}) collective-permute-start(bf16[2,32,462]{2,1,0:T(8,128)(2,1)S(1)} %pad_maximum_fusion.4), channel_id=1, source_target_pairs={{0,3},{1,0},{2,1},{3,2},{4,7},{5,4},{6,5},{7,6},{8,11},{9,8},{10,9... | collective-permute-start | bytes 177416 | tf_op jit(solution)/shard_map/ppermute | solution.py:29
  44.1 7.8 %collective-permute-start.9 = (bf16[64,2048]{1,0:T(8,128)(2,1)}, bf16[64,2048]{1,0:T(8,128)(2,1)}, u32[]{:S(2)}, u32[]{:S(2)}) collective-permute-start(bf16[64,2048]{1,0:T(8,128)(2,1)} %get-tuple-element.60), channel_id=1, source_target_pairs={{0,3},{1,0},{2,1},{3,2},{4,7},{5,4},{6,5},{7,6},{8,11},{9,8},{10,9... | collective-permute-start | bytes 786440 | tf_op jit(solution)/shard_map/ppermute | solution.py:29
  47.7 7.9 %collective-permute-start.10 = (bf16[64,2048]{1,0:T(8,128)(2,1)}, bf16[64,2048]{1,0:T(8,128)(2,1)}, u32[]{:S(2)}, u32[]{:S(2)}) collective-permute-start(bf16[64,2048]{1,0:T(8,128)(2,1)} %get-tuple-element.61), channel_id=1, source_target_pairs={{0,1},{1,2},{2,3},{3,0},{4,5},{5,6},{6,7},{7,4},{8,9},{9,10},{10,1... | collective-permute-start | bytes 786440 | tf_op jit(solution)/shard_map/ppermute | solution.py:29
  62.0 10.7 %collective-permute-start.11 = (bf16[4,64,462]{2,1,0:T(8,128)(2,1)S(1)}, bf16[4,64,462]{2,1,0:T(8,128)(2,1)S(1)}, u32[]{:S(2)}, u32[]{:S(2)}) collective-permute-start(bf16[4,64,462]{2,1,0:T(8,128)(2,1)S(1)} %get-tuple-element.68), channel_id=1, source_target_pairs={{0,8},{8,16},{16,24},{24,0},{1,9},{9,17},{17,25},{25,1},{2,10},{10... | collective-permute-start | bytes 709640 | tf_op jit(solution)/shard_map/ppermute | solution.py:29
  63.7 12.0 %collective-permute-start.12 = (bf16[4,64,462]{2,1,0:T(8,128)(2,1)S(1)}, bf16[4,64,462]{2,1,0:T(8,128)(2,1)S(1)}, u32[]{:S(2)}, u32[]{:S(2)}) collective-permute-start(bf16[4,64,462]{2,1,0:T(8,128)(2,1)S(1)} %get-tuple-element.69), channel_id=1, source_target_pairs={{0,16},{8,24},{16,0},{24,8},{1,17},{9,25},{17,1},{25,9},{2,18},{10... | collective-permute-start | bytes 709640 | tf_op jit(solution)/shard_map/ppermute | solution.py:29
  66.6 9.1 %collective-permute-start.13 = (bf16[4,64,462]{2,1,0:T(8,128)(2,1)S(1)}, bf16[4,64,462]{2,1,0:T(8,128)(2,1)S(1)}, u32[]{:S(2)}, u32[]{:S(2)}) collective-permute-start(bf16[4,64,462]{2,1,0:T(8,128)(2,1)S(1)} %get-tuple-element.70), channel_id=1, source_target_pairs={{0,24},{8,0},{16,8},{24,16},{1,25},{9,1},{17,9},{25,17},{2,26},{10... | collective-permute-start | bytes 709640 | tf_op jit(solution)/shard_map/ppermute | solution.py:29
  75.7 12.4 %collective-permute-start.14 = (bf16[4,64,462]{2,1,0:T(8,128)(2,1)S(1)}, bf16[4,64,462]{2,1,0:T(8,128)(2,1)S(1)}, u32[]{:S(2)}, u32[]{:S(2)}) collective-permute-start(bf16[4,64,462]{2,1,0:T(8,128)(2,1)S(1)} %get-tuple-element.81), channel_id=1, source_target_pairs={{0,8},{8,16},{16,24},{24,0},{1,9},{9,17},{17,25},{25,1},{2,10},{10... | collective-permute-start | bytes 709640 | tf_op jit(solution)/shard_map/ppermute | solution.py:29
  79.8 13.9 %collective-permute-start.15 = (bf16[4,64,462]{2,1,0:T(8,128)(2,1)S(1)}, bf16[4,64,462]{2,1,0:T(8,128)(2,1)S(1)}, u32[]{:S(2)}, u32[]{:S(2)}) collective-permute-start(bf16[4,64,462]{2,1,0:T(8,128)(2,1)S(1)} %get-tuple-element.82), channel_id=1, source_target_pairs={{0,16},{8,24},{16,0},{24,8},{1,17},{9,25},{17,1},{25,9},{2,18},{10... | collective-permute-start | bytes 709640 | tf_op jit(solution)/shard_map/ppermute | solution.py:29
  80.8 12.9 %collective-permute-start.16 = (bf16[4,64,462]{2,1,0:T(8,128)(2,1)S(1)}, bf16[4,64,462]{2,1,0:T(8,128)(2,1)S(1)}, u32[]{:S(2)}, u32[]{:S(2)}) collective-permute-start(bf16[4,64,462]{2,1,0:T(8,128)(2,1)S(1)} %get-tuple-element.83), channel_id=1, source_target_pairs={{0,24},{8,0},{16,8},{24,16},{1,25},{9,1},{17,9},{25,17},{2,26},{10... | collective-permute-start | bytes 709640 | tf_op jit(solution)/shard_map/ppermute | solution.py:29
  83.8 15.8 %collective-permute-start.19 = (bf16[4,64,462]{2,1,0:T(8,128)(2,1)S(1)}, bf16[4,64,462]{2,1,0:T(8,128)(2,1)S(1)}, u32[]{:S(2)}, u32[]{:S(2)}) collective-permute-start(bf16[4,64,462]{2,1,0:T(8,128)(2,1)S(1)} %gradient0.1.own), channel_id=1, source_target_pairs={{0,24},{8,0},{16,8},{24,16},{1,25},{9,1},{17,9},{25,17},{2,26},{10... | collective-permute-start | bytes 709640 | tf_op jit(solution)/shard_map/ppermute | solution.py:29
  85.3 16.0 %collective-permute-start.18 = (bf16[4,64,462]{2,1,0:T(8,128)(2,1)S(1)}, bf16[4,64,462]{2,1,0:T(8,128)(2,1)S(1)}, u32[]{:S(2)}, u32[]{:S(2)}) collective-permute-start(bf16[4,64,462]{2,1,0:T(8,128)(2,1)S(1)} %gradient0.1.own), channel_id=1, source_target_pairs={{0,16},{8,24},{16,0},{24,8},{1,17},{9,25},{17,1},{25,9},{2,18},{10... | collective-permute-start | bytes 709640 | tf_op jit(solution)/shard_map/ppermute | solution.py:29
  88.1 13.7 %collective-permute-start.17 = (bf16[4,64,462]{2,1,0:T(8,128)(2,1)S(1)}, bf16[4,64,462]{2,1,0:T(8,128)(2,1)S(1)}, u32[]{:S(2)}, u32[]{:S(2)}) collective-permute-start(bf16[4,64,462]{2,1,0:T(8,128)(2,1)S(1)} %gradient0.1.own), channel_id=1, source_target_pairs={{0,8},{8,16},{16,24},{24,0},{1,9},{9,17},{17,25},{25,1},{2,10},{10... | collective-permute-start | bytes 709640 | tf_op jit(solution)/shard_map/ppermute | solution.py:29
  95.0 17.3 %collective-permute-start.22 = (bf16[4,64,462]{2,1,0:T(8,128)(2,1)S(1)}, bf16[4,64,462]{2,1,0:T(8,128)(2,1)S(1)}, u32[]{:S(2)}, u32[]{:S(2)}) collective-permute-start(bf16[4,64,462]{2,1,0:T(8,128)(2,1)S(1)} %gradient1.1.own), channel_id=1, source_target_pairs={{0,24},{8,0},{16,8},{24,16},{1,25},{9,1},{17,9},{25,17},{2,26},{10... | collective-permute-start | bytes 709640 | tf_op jit(solution)/shard_map/ppermute | solution.py:29
  97.1 15.1 %collective-permute-start.21 = (bf16[4,64,462]{2,1,0:T(8,128)(2,1)S(1)}, bf16[4,64,462]{2,1,0:T(8,128)(2,1)S(1)}, u32[]{:S(2)}, u32[]{:S(2)}) collective-permute-start(bf16[4,64,462]{2,1,0:T(8,128)(2,1)S(1)} %gradient1.1.own), channel_id=1, source_target_pairs={{0,16},{8,24},{16,0},{24,8},{1,17},{9,25},{17,1},{25,9},{2,18},{10... | collective-permute-start | bytes 709640 | tf_op jit(solution)/shard_map/ppermute | solution.py:29
  99.6 12.7 %collective-permute-start.20 = (bf16[4,64,462]{2,1,0:T(8,128)(2,1)S(1)}, bf16[4,64,462]{2,1,0:T(8,128)(2,1)S(1)}, u32[]{:S(2)}, u32[]{:S(2)}) collective-permute-start(bf16[4,64,462]{2,1,0:T(8,128)(2,1)S(1)} %gradient1.1.own), channel_id=1, source_target_pairs={{0,8},{8,16},{16,24},{24,0},{1,9},{9,17},{17,25},{25,1},{2,10},{10... | collective-permute-start | bytes 709640 | tf_op jit(solution)/shard_map/ppermute | solution.py:29
  107.1 10.8 %collective-permute-start.23 = (bf16[64,2048]{1,0:T(8,128)(2,1)S(1)}, bf16[64,2048]{1,0:T(8,128)(2,1)S(1)}, u32[]{:S(2)}, u32[]{:S(2)}) collective-permute-start(bf16[64,2048]{1,0:T(8,128)(2,1)S(1)} %get-tuple-element.90), channel_id=1, source_target_pairs={{0,1},{1,2},{2,3},{3,0},{4,5},{5,6},{6,7},{7,4},{8,9},{9,10},{10,1... | collective-permute-start | bytes 786440 | tf_op jit(solution)/shard_map/ppermute | solution.py:29
  107.1 14.2 %collective-permute-start.24 = (bf16[64,2048]{1,0:T(8,128)(2,1)S(1)}, bf16[64,2048]{1,0:T(8,128)(2,1)S(1)}, u32[]{:S(2)}, u32[]{:S(2)}) collective-permute-start(bf16[64,2048]{1,0:T(8,128)(2,1)S(1)} %get-tuple-element.91), channel_id=1, source_target_pairs={{0,2},{1,3},{2,0},{3,1},{4,6},{5,7},{6,4},{7,5},{8,10},{9,11},{10,... | collective-permute-start | bytes 786440 | tf_op jit(solution)/shard_map/ppermute | solution.py:29
  112.2 9.1 %collective-permute-start.25 = (bf16[64,2048]{1,0:T(8,128)(2,1)S(1)}, bf16[64,2048]{1,0:T(8,128)(2,1)S(1)}, u32[]{:S(2)}, u32[]{:S(2)}) collective-permute-start(bf16[64,2048]{1,0:T(8,128)(2,1)S(1)} %get-tuple-element.92), channel_id=1, source_target_pairs={{0,3},{1,0},{2,1},{3,2},{4,7},{5,4},{6,5},{7,6},{8,11},{9,8},{10,9... | collective-permute-start | bytes 786440 | tf_op jit(solution)/shard_map/ppermute | solution.py:29
  116.8 23.7 %collective-permute-start.29 = (bf16[256,2048]{1,0:T(8,128)(2,1)}, bf16[256,2048]{1,0:T(8,128)(2,1)S(1)}, u32[]{:S(2)}, u32[]{:S(2)}) collective-permute-start(bf16[256,2048]{1,0:T(8,128)(2,1)} %get-tuple-element.102.refs_0_), channel_id=1, source_target_pairs={{0,32},{32,0},{1,33},{33,1},{2,34},{34,2},{3,35},{35,3},{4,36},{36... | collective-permute-start | bytes 3145736 | tf_op jit(solution)/shard_map/ppermute | solution.py:29
  116.9 23.6 %collective-permute-start.30 = (bf16[256,2048]{1,0:T(8,128)(2,1)}, bf16[256,2048]{1,0:T(8,128)(2,1)S(1)}, u32[]{:S(2)}, u32[]{:S(2)}) collective-permute-start(bf16[256,2048]{1,0:T(8,128)(2,1)} %get-tuple-element.103.refs_1_), channel_id=1, source_target_pairs={{0,32},{32,0},{1,33},{33,1},{2,34},{34,2},{3,35},{35,3},{4,36},{36... | collective-permute-start | bytes 3145736 | tf_op jit(solution)/shard_map/ppermute | solution.py:29
  121.3 9.5 %collective-permute-start.26 = (bf16[64,2048]{1,0:T(8,128)(2,1)S(1)}, bf16[64,2048]{1,0:T(8,128)(2,1)S(1)}, u32[]{:S(2)}, u32[]{:S(2)}) collective-permute-start(bf16[64,2048]{1,0:T(8,128)(2,1)S(1)} %get-tuple-element.97), channel_id=1, source_target_pairs={{0,1},{1,2},{2,3},{3,0},{4,5},{5,6},{6,7},{7,4},{8,9},{9,10},{10,1... | collective-permute-start | bytes 786440 | tf_op jit(solution)/shard_map/ppermute | solution.py:29
  121.3 13.8 %collective-permute-start.27 = (bf16[64,2048]{1,0:T(8,128)(2,1)S(1)}, bf16[64,2048]{1,0:T(8,128)(2,1)S(1)}, u32[]{:S(2)}, u32[]{:S(2)}) collective-permute-start(bf16[64,2048]{1,0:T(8,128)(2,1)S(1)} %get-tuple-element.98), channel_id=1, source_target_pairs={{0,2},{1,3},{2,0},{3,1},{4,6},{5,7},{6,4},{7,5},{8,10},{9,11},{10,... | collective-permute-start | bytes 786440 | tf_op jit(solution)/shard_map/ppermute | solution.py:29
  124.8 10.3 %collective-permute-start.28 = (bf16[64,2048]{1,0:T(8,128)(2,1)S(1)}, bf16[64,2048]{1,0:T(8,128)(2,1)S(1)}, u32[]{:S(2)}, u32[]{:S(2)}) collective-permute-start(bf16[64,2048]{1,0:T(8,128)(2,1)S(1)} %get-tuple-element.99), channel_id=1, source_target_pairs={{0,3},{1,0},{2,1},{3,2},{4,7},{5,4},{6,5},{7,6},{8,11},{9,8},{10,9... | collective-permute-start | bytes 786440 | tf_op jit(solution)/shard_map/ppermute | solution.py:29
  130.8 9.7 %collective-permute-start.31 = (bf16[2,4,64,462]{3,2,1,0:T(8,128)(2,1)S(1)}, bf16[2,4,64,462]{3,2,1,0:T(8,128)(2,1)}, u32[]{:S(2)}, u32[]{:S(2)}) collective-permute-start(bf16[2,4,64,462]{3,2,1,0:T(8,128)(2,1)S(1)} %get-tuple-element.106), channel_id=1, source_target_pairs={{0,32},{32,0},{1,33},{33,1},{2,34},{34,2},{3,35},{35,3},{4,36},{36... | collective-permute-start | bytes 1419272 | tf_op jit(solution)/shard_map/ppermute | solution.py:29
  136.1 20.6 %all-to-all-start.1 = ((bf16[8,16,2048]{2,1,0:T(8,128)(2,1)}), bf16[8,16,2048]{2,1,0:T(8,128)(2,1)}, u32[]{:S(2)}, u32[]{:S(2)}) async-start(bf16[8,16,2048]{2,1,0:T(8,128)(2,1)} %bitcast.28), calls=%async_computation.1 | async-start | bytes 1048576 | tf_op jit(solution)/shard_map/all_to_all | solution.py:45
  (11 other events, 98.1 us)
where the time goes:
time: 159 us
  starting transfers between devices  55.8 us (35%)
  waiting for transfers between devices  53 us (33%)
  Pallas kernels  32.6 us (21%)
  local copies, waits for them, and re-layouts  11.5 us (7%)
  other arithmetic  4.68 us (3%)
    ppermute x33, starting transfers between devices, shift(): lax.ppermute(value, axis, [(i, (i + by) % size) for i in range(size)])  42.9 us
    ppermute x33, waiting for transfers between devices, shift(): lax.ppermute(value, axis, [(i, (i + by) % size) for i in range(size)])  37.7 us
    all_to_all x2, waiting for transfers between devices, exchange(): return lax.all_to_all(value, axes, split_axis=0, concat_axis=0, tiled=True)  15.3 us
    all_to_all x2, starting transfers between devices, exchange(): return lax.all_to_all(value, axes, split_axis=0, concat_axis=0, tiled=True)  12.9 us
    pallas_call x2, Pallas kernels, weight_grad(): pl.pallas_call(functools.partial(weights_kernel, side, min(512, width)),...  10.5 us
    pallas_call x2, Pallas kernels, forward(): pl.pallas_call(functools.partial(forward_kernel, half), out_shape=(jax.Sh...  9.68 us
    pallas_call x2, Pallas kernels, backward(): pl.pallas_call(functools.partial(backward_kernel, min(512, width)), out_s...  9.05 us
    unnamed x17, local copies, waits for them, and re-layouts  5.56 us
  transfers between devices with their start and end apart: 35, of which 16 were waited for; matrix products, arithmetic and copies ran while one was open for 6% of the time, Pallas kernels for 18%

commit v1 on v0

--- a/solution.py
+++ b/solution.py
@@ -167,30 +167,31 @@
     )(at, *pieces, *weights)
 
 
-def weights_kernel(side, tile, *refs):
-    n = len(refs) // 2
-    tokens, fulls, out = refs[:n], refs[n : 2 * n], refs[-1]
-    rows = jnp.concatenate([f[side].reshape(NX * PART, out.shape[0]) for f in fulls], axis=0)
-    for col in range(0, out.shape[1], tile):
-        total = lax.dot_general(
-            rows,
-            jnp.concatenate([r[:, col : col + tile] for r in tokens], axis=0),
-            (((0,), (0,)), ((), ())),
-            preferred_element_type=F32,
-        )
-        out[:, col : col + tile] = total.astype(BF16)
-
-
-def weight_grad(tokens, fulls, side):
+def weights_kernel(tile, *refs):
+    tokens, fulls, outs = refs[:4], refs[4:8], refs[8:]
+    for side, out in enumerate(outs):
+        rows = jnp.concatenate([f[side].reshape(NX * PART, out.shape[0]) for f in fulls], axis=0)
+        for col in range(0, out.shape[1], tile):
+            total = lax.dot_general(
+                rows,
+                jnp.concatenate([r[:, col : col + tile] for r in tokens], axis=0),
+                (((0,), (0,)), ((), ())),
+                preferred_element_type=F32,
+            )
+            out[:, col : col + tile] = total.astype(BF16)
+
+
+def weight_grads(tokens, fulls):
     width = tokens[0].shape[1]
-    return pl.pallas_call(
-        functools.partial(weights_kernel, side, min(512, width)),
-        out_shape=jax.ShapeDtypeStruct((fulls[0].shape[3], width), BF16),
-        in_specs=[VMEM] * (2 * len(tokens)),
-        out_specs=VMEM,
-        compiler_params=PARAMS,
-        cost_estimate=cost(5),
-        name="weight_grad%d" % side,
+    out = jax.ShapeDtypeStruct((fulls[0].shape[3], width), BF16)
+    return pl.pallas_call(
+        functools.partial(weights_kernel, min(512, width)),
+        out_shape=(out, out),
+        in_specs=[VMEM] * 8,
+        out_specs=(VMEM, VMEM),
+        compiler_params=PARAMS,
+        cost_estimate=cost(10),
+        name="weight_grads",
     )(*tokens, *fulls)
 
 
@@ -211,6 +212,25 @@
         cost_estimate=cost(0.1),
         name="halves",
     )(a, b)
+
+
+def add_up_kernel(got, out):
+    total = got[0].astype(F32)
+    for z in range(1, got.shape[0]):
+        total = total + got[z].astype(F32)
+    out[...] = total.astype(BF16)
+
+
+def add_up(got):
+    return pl.pallas_call(
+        add_up_kernel,
+        out_shape=jax.ShapeDtypeStruct(got.shape[1:], BF16),
+        in_specs=[VMEM],
+        out_specs=VMEM,
+        compiler_params=PARAMS,
+        cost_estimate=cost(0.1),
+        name="add_up",
+    )(got)
 
 
 def local(acts, gate_weight, up_weight, hidden_grad):
@@ -252,7 +272,7 @@
     full0, passed0, kept0, *parts0 = backward(after(at, grad1), 0, pieces0, weights)
     sums0 = [x_shift(part, o) for o, part in enumerate(parts0, 1)]
     full1, passed1, kept1, *parts1 = backward(after(at, kept0), 1, pieces1, weights)
-    parts1, sums0 = lax.optimization_barrier((parts1, sums0))
+    parts1, sums0[0], sums0[2] = lax.optimization_barrier((parts1, sums0[0], sums0[2]))
     sums1 = [x_shift(part, o) for o, part in enumerate(parts1, 1)]
 
     totals = []
@@ -265,9 +285,9 @@
     tokens0, tokens1, kept1 = lax.optimization_barrier((tokens0, tokens1, kept1))
     tokens = [tokens0, tokens1, core_swap(tokens0), core_swap(tokens1)]
     fulls = [full0, full1, core_swap(passed0), core_swap(passed1)]
-    gate_weight_grad, up_weight_grad = [weight_grad(tokens, fulls, side) for side in (0, 1)]
+    gate_weight_grad, up_weight_grad = weight_grads(tokens, fulls)
     got, gate_weight_grad, up_weight_grad = lax.optimization_barrier((got, gate_weight_grad, up_weight_grad))
-    input_grad = got.astype(F32).sum(axis=0).astype(BF16)
+    input_grad = add_up(got)
     return input_grad, gate_weight_grad, up_weight_grad
 
 

time: 159 us -> 157 us (0.987)
  starting transfers between devices: 55.8 us -> 58.8 us
  Pallas kernels: 32.6 us -> 30.7 us
  other arithmetic: 4.68 us -> 2.9 us
    ppermute x33, waiting for transfers between devices: 37.7 us -> 33.6 us  [shift(): lax.ppermute(value, axis, [(i, (i + by) % size) for i in range(size)])]
    all_to_all x2, waiting for transfers between devices: 15.3 us -> 18.1 us  [exchange(): return lax.all_to_all(value, axes, split_axis=0, concat_axis=0, tiled=True)]
    pallas_call x2, Pallas kernels: 10.5 us -> 8.2 us  [the longest x1 7.5 us: weight_grads(): pl.pallas_call(functools.partial(weights_kernel, min(512, width)), out_sh...]
    ppermute x33, starting transfers between devices: 42.9 us -> 45 us  [shift(): lax.ppermute(value, axis, [(i, (i + by) % size) for i in range(size)])]
    reduce_sum x1 -> x0, other arithmetic: 1.76 us -> none  [local(): input_grad = got.astype(F32).sum(axis=0).astype(BF16)]
  transfers between devices with their start and end apart: 35 -> 35, of which waited for: 16 -> 15; matrix products, arithmetic and copies ran while one was open for 6% -> 6% of each run, Pallas kernels for 18% -> 16%
where the time goes in v1:
time: 157 us
  starting transfers between devices  58.8 us (37%)
  waiting for transfers between devices  51.8 us (33%)
  Pallas kernels  30.7 us (20%)
  local copies, waits for them, and re-layouts  11.5 us (7%)
  other arithmetic  2.9 us (2%)
    ppermute x33, starting transfers between devices, shift(): lax.ppermute(value, axis, [(i, (i + by) % size) for i in range(size)])  45 us
    ppermute x33, waiting for transfers between devices, shift(): lax.ppermute(value, axis, [(i, (i + by) % size) for i in range(size)])  33.6 us
    all_to_all x2, waiting for transfers between devices, exchange(): return lax.all_to_all(value, axes, split_axis=0, concat_axis=0, tiled=True)  18.1 us
    all_to_all x2, starting transfers between devices, exchange(): return lax.all_to_all(value, axes, split_axis=0, concat_axis=0, tiled=True)  13.8 us
    pallas_call x2, Pallas kernels, forward(): pl.pallas_call(functools.partial(forward_kernel, half), out_shape=(jax.Sh...  9.68 us
    pallas_call x2, Pallas kernels, backward(): pl.pallas_call(functools.partial(backward_kernel, min(512, width)), out_s...  9.42 us
    pallas_call x1, Pallas kernels, weight_grads(): pl.pallas_call(functools.partial(weights_kernel, min(512, width)), out_sh...  7.5 us
    unnamed x17, local copies, waits for them, and re-layouts  5.56 us
  transfers between devices with their start and end apart: 35, of which 15 were waited for; matrix products, arithmetic and copies ran while one was open for 6% of the time, Pallas kernels for 16%

profile of v1, /device:TPU:32, one launch (start us, length us, event | category | flops | bytes accessed | tf_op | source)
XLA Modules:
  0.0 156.5 jit_solution(1062550474584919947)
XLA Ops:
  1.2 1.7 %broadcast_in_dim.2 = bf16[8,16,2048]{2,1,0:T(8,128)(2,1)} broadcast(bf16[16,2048]{1,0:T(8,128)(2,1)} %param.4), dimensions={1,2} | broadcast | bytes 589824 | tf_op jit(solution)/shard_map/broadcast_in_dim | solution.py:248
  2.9 8.6 %all-to-all-start = ((bf16[8,16,2048]{2,1,0:T(8,128)(2,1)}), bf16[8,16,2048]{2,1,0:T(8,128)(2,1)S(1)}, u32[]{:S(2)}, u32[]{:S(2)}) async-start(bf16[8,16,2048]{2,1,0:T(8,128)(2,1)} %broadcast_in_dim.2), calls=%async_computation | async-start | bytes 1048576 | tf_op jit(solution)/shard_map/all_to_all | solution.py:45
  12.7 2.3 %reshape.21 = bf16[2,4,16,2,4,462]{5,4,3,2,1,0:T(4,128)(2,1)S(1)} reshape(bf16[128,3696]{1,0:T(8,128)(2,1)S(1)} %copy.8) | data formatting | bytes 1892352 | tf_op jit(solution)/shard_map/reshape | solution.py:244
  16.1 11.6 %all-to-all-done = bf16[8,16,2048]{2,1,0:T(8,128)(2,1)S(1)} async-done(((bf16[8,16,2048]{2,1,0:T(8,128)(2,1)}), bf16[8,16,2048]{2,1,0:T(8,128)(2,1)S(1)}, u32[]{:S(2)}, u32[]{:S(2)}) %all-to-all-start) | async-done | bytes 524320 | tf_op jit(solution)/shard_map/all_to_all | solution.py:45
  29.3 1.7 %collective-permute-start.7 = (bf16[128,2048]{1,0:T(8,128)(2,1)S(1)}, bf16[128,2048]{1,0:T(8,128)(2,1)S(1)}, u32[]{:S(2)}, u32[]{:S(2)}) collective-permute-start(bf16[128,2048]{1,0:T(8,128)(2,1)S(1)} %bitcast.25), channel_id=1, source_target_pairs={{0,3},{1,0},{2,1},{3,2},{4,7},{5,4},{6,5},{7,6},{8,11},{9,8},{10,9... | collective-permute-start | bytes 1572872 | tf_op jit(solution)/shard_map/ppermute | solution.py:29
  32.9 4.1 %collective-permute-done.2 = bf16[4,32,462]{2,1,0:T(8,128)(2,1)S(1)} collective-permute-done((bf16[4,32,462]{2,1,0:T(8,128)(2,1)S(1)}, bf16[4,32,462]{2,1,0:T(8,128)(2,1)S(1)}, u32[]{:S(2)}, u32[]{:S(2)}) %collective-permute-start.2) | collective-permute-done | bytes 118304 | tf_op jit(solution)/shard_map/ppermute | solution.py:29
  37.4 2.8 %collective-permute-start.4 = (bf16[2,32,462]{2,1,0:T(8,128)(2,1)S(1)}, bf16[2,32,462]{2,1,0:T(8,128)(2,1)S(1)}, u32[]{:S(2)}, u32[]{:S(2)}) collective-permute-start(bf16[2,32,462]{2,1,0:T(8,128)(2,1)S(1)} %pad_maximum_fusion.3), channel_id=1, source_target_pairs={{0,2},{1,3},{2,0},{3,1},{4,6},{5,7},{6,4},{7,5},{8,10},{9,11},{10,... | collective-permute-start | bytes 177416 | tf_op jit(solution)/shard_map/ppermute | solution.py:29
  44.1 3.6 %collective-permute-start.9 = (bf16[64,2048]{1,0:T(8,128)(2,1)}, bf16[64,2048]{1,0:T(8,128)(2,1)}, u32[]{:S(2)}, u32[]{:S(2)}) collective-permute-start(bf16[64,2048]{1,0:T(8,128)(2,1)} %get-tuple-element.61), channel_id=1, source_target_pairs={{0,3},{1,0},{2,1},{3,2},{4,7},{5,4},{6,5},{7,6},{8,11},{9,8},{10,9... | collective-permute-start | bytes 786440 | tf_op jit(solution)/shard_map/ppermute | solution.py:29
  48.5 1.8 %collective-permute-done.6.cot_sibling = bf16[4,2,32,462]{3,2,1,0:T(8,128)(2,1)} collective-permute-done((bf16[4,2,32,462]{3,2,1,0:T(8,128)(2,1)}, bf16[4,2,32,462]{3,2,1,0:T(8,128)(2,1)}, u32[]{:S(2)}, u32[]{:S(2)}) %collective-permute-start.6) | collective-permute-done | bytes 236576 | tf_op jit(solution)/shard_map/ppermute | solution.py:29
  50.3 1.5 collective-permute-done.9.refs_2_
  51.9 3.7 %collective-permute-done.10.refs_2_ = bf16[64,2048]{1,0:T(8,128)(2,1)} collective-permute-done((bf16[64,2048]{1,0:T(8,128)(2,1)}, bf16[64,2048]{1,0:T(8,128)(2,1)}, u32[]{:S(2)}, u32[]{:S(2)}) %collective-permute-start.10) | collective-permute-done | bytes 262176 | tf_op jit(solution)/shard_map/ppermute | solution.py:29
  55.6 1.5 copy-done.1
  57.1 4.9 %forward0.1 = (bf16[256,2048]{1,0:T(8,128)(2,1)}, f32[4,64,462]{2,1,0:T(8,128)S(1)}, bf16[4,64,462]{2,1,0:T(8,128)(2,1)S(1)}, bf16[4,64,462]{2,1,0:T(8,128)(2,1)S(1)}, bf16[4,64,462]{2,1,0:T(8,128)(2,1)S(1)}) custom-call(s32[4]{0:T(128)S(1)} %pad_add_fusion.at_ref, bf16[128,2048]{1,0:T(8,128)(2,1)S(1)} %bitcast.26, ...), custom_call_target="tpu_custom_call" | custom-call | flops 110000000 | bytes 1 | tf_op jit(solution)/shard_map/forward0/pallas_call | solution.py:82
  62.0 1.6 %collective-permute-start.11 = (bf16[4,64,462]{2,1,0:T(8,128)(2,1)S(1)}, bf16[4,64,462]{2,1,0:T(8,128)(2,1)S(1)}, u32[]{:S(2)}, u32[]{:S(2)}) collective-permute-start(bf16[4,64,462]{2,1,0:T(8,128)(2,1)S(1)} %get-tuple-element.69), channel_id=1, source_target_pairs={{0,8},{8,16},{16,24},{24,0},{1,9},{9,17},{17,25},{25,1},{2,10},{10... | collective-permute-start | bytes 709640 | tf_op jit(solution)/shard_map/ppermute | solution.py:29
  63.7 2.9 %collective-permute-start.12 = (bf16[4,64,462]{2,1,0:T(8,128)(2,1)S(1)}, bf16[4,64,462]{2,1,0:T(8,128)(2,1)S(1)}, u32[]{:S(2)}, u32[]{:S(2)}) collective-permute-start(bf16[4,64,462]{2,1,0:T(8,128)(2,1)S(1)} %get-tuple-element.70), channel_id=1, source_target_pairs={{0,16},{8,24},{16,0},{24,8},{1,17},{9,25},{17,1},{25,9},{2,18},{10... | collective-permute-start | bytes 709640 | tf_op jit(solution)/shard_map/ppermute | solution.py:29
  67.9 4.8 %forward1.1 = (bf16[256,2048]{1,0:T(8,128)(2,1)}, f32[4,64,462]{2,1,0:T(8,128)S(1)}, bf16[4,64,462]{2,1,0:T(8,128)(2,1)S(1)}, bf16[4,64,462]{2,1,0:T(8,128)(2,1)S(1)}, bf16[4,64,462]{2,1,0:T(8,128)(2,1)S(1)}) custom-call(s32[4]{0:T(128)S(1)} %pad_add_fusion.at_ref, bf16[128,2048]{1,0:T(8,128)(2,1)S(1)} %bitcast.27, ...), custom_call_target="tpu_custom_call" | custom-call | flops 110000000 | bytes 1 | tf_op jit(solution)/shard_map/forward1/pallas_call | solution.py:82
  72.7 3.0 %collective-permute-done.12.from2 = bf16[4,64,462]{2,1,0:T(8,128)(2,1)S(1)} collective-permute-done((bf16[4,64,462]{2,1,0:T(8,128)(2,1)S(1)}, bf16[4,64,462]{2,1,0:T(8,128)(2,1)S(1)}, u32[]{:S(2)}, u32[]{:S(2)}) %collective-permute-start.12) | collective-permute-done | bytes 236576 | tf_op jit(solution)/shard_map/ppermute | solution.py:29
  75.7 4.1 %collective-permute-start.14 = (bf16[4,64,462]{2,1,0:T(8,128)(2,1)S(1)}, bf16[4,64,462]{2,1,0:T(8,128)(2,1)S(1)}, u32[]{:S(2)}, u32[]{:S(2)}) collective-permute-start(bf16[4,64,462]{2,1,0:T(8,128)(2,1)S(1)} %get-tuple-element.82), channel_id=1, source_target_pairs={{0,8},{8,16},{16,24},{24,0},{1,9},{9,17},{17,25},{25,1},{2,10},{10... | collective-permute-start | bytes 709640 | tf_op jit(solution)/shard_map/ppermute | solution.py:29
  80.8 1.7 %collective-permute-start.16 = (bf16[4,64,462]{2,1,0:T(8,128)(2,1)S(1)}, bf16[4,64,462]{2,1,0:T(8,128)(2,1)S(1)}, u32[]{:S(2)}, u32[]{:S(2)}) collective-permute-start(bf16[4,64,462]{2,1,0:T(8,128)(2,1)S(1)} %get-tuple-element.84), channel_id=1, source_target_pairs={{0,24},{8,0},{16,8},{24,16},{1,25},{9,1},{17,9},{25,17},{2,26},{10... | collective-permute-start | bytes 709640 | tf_op jit(solution)/shard_map/ppermute | solution.py:29
  86.3 1.8 %collective-permute-done.14.from1 = bf16[4,64,462]{2,1,0:T(8,128)(2,1)S(1)} collective-permute-done((bf16[4,64,462]{2,1,0:T(8,128)(2,1)S(1)}, bf16[4,64,462]{2,1,0:T(8,128)(2,1)S(1)}, u32[]{:S(2)}, u32[]{:S(2)}) %collective-permute-start.14) | collective-permute-done | bytes 236576 | tf_op jit(solution)/shard_map/ppermute | solution.py:29
  88.1 5.6 %collective-permute-done.15.from2 = bf16[4,64,462]{2,1,0:T(8,128)(2,1)S(1)} collective-permute-done((bf16[4,64,462]{2,1,0:T(8,128)(2,1)S(1)}, bf16[4,64,462]{2,1,0:T(8,128)(2,1)S(1)}, u32[]{:S(2)}, u32[]{:S(2)}) %collective-permute-start.15) | collective-permute-done | bytes 236576 | tf_op jit(solution)/shard_map/ppermute | solution.py:29
  95.0 2.1 %collective-permute-start.22 = (bf16[4,64,462]{2,1,0:T(8,128)(2,1)S(1)}, bf16[4,64,462]{2,1,0:T(8,128)(2,1)S(1)}, u32[]{:S(2)}, u32[]{:S(2)}) collective-permute-start(bf16[4,64,462]{2,1,0:T(8,128)(2,1)S(1)} %gradient1.1.own), channel_id=1, source_target_pairs={{0,24},{8,0},{16,8},{24,16},{1,25},{9,1},{17,9},{25,17},{2,26},{10... | collective-permute-start | bytes 709640 | tf_op jit(solution)/shard_map/ppermute | solution.py:29
  97.1 2.4 %collective-permute-start.21 = (bf16[4,64,462]{2,1,0:T(8,128)(2,1)S(1)}, bf16[4,64,462]{2,1,0:T(8,128)(2,1)S(1)}, u32[]{:S(2)}, u32[]{:S(2)}) collective-permute-start(bf16[4,64,462]{2,1,0:T(8,128)(2,1)S(1)} %gradient1.1.own), channel_id=1, source_target_pairs={{0,16},{8,24},{16,0},{24,8},{1,17},{9,25},{17,1},{25,9},{2,18},{10... | collective-permute-start | bytes 709640 | tf_op jit(solution)/shard_map/ppermute | solution.py:29
  99.6 1.7 %collective-permute-start.20 = (bf16[4,64,462]{2,1,0:T(8,128)(2,1)S(1)}, bf16[4,64,462]{2,1,0:T(8,128)(2,1)S(1)}, u32[]{:S(2)}, u32[]{:S(2)}) collective-permute-start(bf16[4,64,462]{2,1,0:T(8,128)(2,1)S(1)} %gradient1.1.own), channel_id=1, source_target_pairs={{0,8},{8,16},{16,24},{24,0},{1,9},{9,17},{17,25},{25,1},{2,10},{10... | collective-permute-start | bytes 709640 | tf_op jit(solution)/shard_map/ppermute | solution.py:29
  101.8 4.5 %backward0.1 = (bf16[2,4,64,462]{3,2,1,0:T(8,128)(2,1)S(1)}, bf16[2,4,64,462]{3,2,1,0:T(8,128)(2,1)S(1)}, f32[64,2048]{1,0:T(8,128)S(1)}, bf16[64,2048]{1,0:T(8,...) custom-call(s32[4]{0:T(128)S(1)} %pad_add_fusion.at_ref, ...), custom_call_target="tpu_custom_call" | custom-call | flops 5500000256 | bytes 1 | tf_op jit(solution)/shard_map/backward0/pallas_call | solution.py:152
  107.1 3.6 %collective-permute-start.24 = (bf16[64,2048]{1,0:T(8,128)(2,1)S(1)}, bf16[64,2048]{1,0:T(8,128)(2,1)S(1)}, u32[]{:S(2)}, u32[]{:S(2)}) collective-permute-start(bf16[64,2048]{1,0:T(8,128)(2,1)S(1)} %get-tuple-element.92), channel_id=1, source_target_pairs={{0,3},{1,0},{2,1},{3,2},{4,7},{5,4},{6,5},{7,6},{8,11},{9,8},{10,9... | collective-permute-start | bytes 786440 | tf_op jit(solution)/shard_map/ppermute | solution.py:29
  112.3 4.9 %backward1.1 = (bf16[2,4,64,462]{3,2,1,0:T(8,128)(2,1)S(1)}, bf16[2,4,64,462]{3,2,1,0:T(8,128)(2,1)}, f32[64,2048]{1,0:T(8,128)S(1)}, bf16[64,2048]{1,0:T(8,128)...) custom-call(s32[4]{0:T(128)S(1)} %pad_add_fusion.at_ref, bf16[4,64,462]{2,1,0:T(8,128)(2,1)S(1)} %gradient1.1.own, ...), custom_call_target="tpu_custom_call" | custom-call | flops 5500000256 | bytes 1 | tf_op jit(solution)/shard_map/backward1/pallas_call | solution.py:152
  119.4 5.1 %collective-permute-start.27 = (bf16[64,2048]{1,0:T(8,128)(2,1)S(1)}, bf16[64,2048]{1,0:T(8,128)(2,1)S(1)}, u32[]{:S(2)}, u32[]{:S(2)}) collective-permute-start(bf16[64,2048]{1,0:T(8,128)(2,1)S(1)} %get-tuple-element.98), channel_id=1, source_target_pairs={{0,2},{1,3},{2,0},{3,1},{4,6},{5,7},{6,4},{7,5},{8,10},{9,11},{10,... | collective-permute-start | bytes 786440 | tf_op jit(solution)/shard_map/ppermute | solution.py:29
  124.7 8.3 %collective-permute-done.26 = bf16[64,2048]{1,0:T(8,128)(2,1)S(1)} collective-permute-done((bf16[64,2048]{1,0:T(8,128)(2,1)S(1)}, bf16[64,2048]{1,0:T(8,128)(2,1)S(1)}, u32[]{:S(2)}, u32[]{:S(2)}) %collective-permute-start.26) | collective-permute-done | bytes 262176 | tf_op jit(solution)/shard_map/ppermute | solution.py:29
  134.5 5.3 %all-to-all-start.1 = ((bf16[8,16,2048]{2,1,0:T(8,128)(2,1)}), bf16[8,16,2048]{2,1,0:T(8,128)(2,1)S(1)}, u32[]{:S(2)}, u32[]{:S(2)}) async-start(bf16[8,16,2048]{2,1,0:T(8,128)(2,1)} %bitcast.28), calls=%async_computation.1 | async-start | bytes 1048576 | tf_op jit(solution)/shard_map/all_to_all | solution.py:45
  141.8 7.5 %weight_grads.1 = (bf16[462,2048]{1,0:T(8,128)(2,1)}, bf16[462,2048]{1,0:T(8,128)(2,1)}) custom-call(bf16[256,2048]{1,0:T(8,128)(2,1)} %get-tuple-element.102.refs_0_, bf16[256,2048]{1,0:T(8,128)(2,1)} %get-tuple-element.103.refs_1_, bf16[256,2048]{1,0:T(8,128)(2,1)S(1)} %collective-permute-done.29.refs_2_, ...), custom_call_target="tpu_custom_call" | custom-call | flops 11000000512 | bytes 1 | tf_op jit(solution)/shard_map/weight_grads/pallas_call | solution.py:187
  149.3 6.5 %all-to-all-done.1.got = bf16[8,16,2048]{2,1,0:T(8,128)(2,1)S(1)} async-done(((bf16[8,16,2048]{2,1,0:T(8,128)(2,1)}), bf16[8,16,2048]{2,1,0:T(8,128)(2,1)S(1)}, u32[]{:S(2)}, u32[]{:S(2)}) %all-to-all-start.1) | async-done | bytes 524320 | tf_op jit(solution)/shard_map/all_to_all | solution.py:45
  (82 shorter events, 28.1 us)
Async XLA Ops:
  0.6 27.2 %collective-permute-start = (bf16[462,2048]{1,0:T(8,128)(2,1)}, bf16[462,2048]{1,0:T(8,128)(2,1)}, u32[]{:S(2)}, u32[]{:S(2)}) collective-permute-start(bf16[462,2048]{1,0:T(8,128)(2,1)} %refs_0_.1), channel_id=1, source_target_pairs={{0,32},{32,0},{1,33},{33,1},{2,34},{34,2},{3,35},{35,3},{4,36},{36... | collective-permute-start | bytes 5677064 | tf_op jit(solution)/shard_map/ppermute | solution.py:29
  0.7 27.1 %collective-permute-start.1 = (bf16[462,2048]{1,0:T(8,128)(2,1)}, bf16[462,2048]{1,0:T(8,128)(2,1)}, u32[]{:S(2)}, u32[]{:S(2)}) collective-permute-start(bf16[462,2048]{1,0:T(8,128)(2,1)} %refs_1_.1), channel_id=1, source_target_pairs={{0,32},{32,0},{1,33},{33,1},{2,34},{34,2},{3,35},{35,3},{4,36},{36... | collective-permute-start | bytes 5677064 | tf_op jit(solution)/shard_map/ppermute | solution.py:29
  2.9 24.9 %all-to-all-start = ((bf16[8,16,2048]{2,1,0:T(8,128)(2,1)}), bf16[8,16,2048]{2,1,0:T(8,128)(2,1)S(1)}, u32[]{:S(2)}, u32[]{:S(2)}) async-start(bf16[8,16,2048]{2,1,0:T(8,128)(2,1)} %broadcast_in_dim.2), calls=%async_computation | async-start | bytes 1048576 | tf_op jit(solution)/shard_map/all_to_all | solution.py:45
  27.8 15.1 %collective-permute-start.8 = (bf16[128,2048]{1,0:T(8,128)(2,1)S(1)}, bf16[128,2048]{1,0:T(8,128)(2,1)S(1)}, u32[]{:S(2)}, u32[]{:S(2)}) collective-permute-start(bf16[128,2048]{1,0:T(8,128)(2,1)S(1)} %bitcast.24), channel_id=1, source_target_pairs={{0,1},{1,2},{2,3},{3,0},{4,5},{5,6},{6,7},{7,4},{8,9},{9,10},{10,1... | collective-permute-start | bytes 1572872 | tf_op jit(solution)/shard_map/ppermute | solution.py:29
  29.3 13.9 %collective-permute-start.7 = (bf16[128,2048]{1,0:T(8,128)(2,1)S(1)}, bf16[128,2048]{1,0:T(8,128)(2,1)S(1)}, u32[]{:S(2)}, u32[]{:S(2)}) collective-permute-start(bf16[128,2048]{1,0:T(8,128)(2,1)S(1)} %bitcast.25), channel_id=1, source_target_pairs={{0,3},{1,0},{2,1},{3,2},{4,7},{5,4},{6,5},{7,6},{8,11},{9,8},{10,9... | collective-permute-start | bytes 1572872 | tf_op jit(solution)/shard_map/ppermute | solution.py:29
  37.0 10.6 %collective-permute-start.3 = (bf16[2,32,462]{2,1,0:T(8,128)(2,1)S(1)}, bf16[2,32,462]{2,1,0:T(8,128)(2,1)S(1)}, u32[]{:S(2)}, u32[]{:S(2)}) collective-permute-start(bf16[2,32,462]{2,1,0:T(8,128)(2,1)S(1)} %pad_maximum_fusion.2), channel_id=1, source_target_pairs={{0,1},{1,2},{2,3},{3,0},{4,5},{5,6},{6,7},{7,4},{8,9},{9,10},{10,1... | collective-permute-start | bytes 177416 | tf_op jit(solution)/shard_map/ppermute | solution.py:29
  37.4 10.3 %collective-permute-start.4 = (bf16[2,32,462]{2,1,0:T(8,128)(2,1)S(1)}, bf16[2,32,462]{2,1,0:T(8,128)(2,1)S(1)}, u32[]{:S(2)}, u32[]{:S(2)}) collective-permute-start(bf16[2,32,462]{2,1,0:T(8,128)(2,1)S(1)} %pad_maximum_fusion.3), channel_id=1, source_target_pairs={{0,2},{1,3},{2,0},{3,1},{4,6},{5,7},{6,4},{7,5},{8,10},{9,11},{10,... | collective-permute-start | bytes 177416 | tf_op jit(solution)/shard_map/ppermute | solution.py:29
  40.2 7.4 %collective-permute-start.5 = (bf16[2,32,462]{2,1,0:T(8,128)(2,1)S(1)}, bf16[2,32,462]{2,1,0:T(8,128)(2,1)S(1)}, u32[]{:S(2)}, u32[]{:S(2)}) collective-permute-start(bf16[2,32,462]{2,1,0:T(8,128)(2,1)S(1)} %pad_maximum_fusion.4), channel_id=1, source_target_pairs={{0,3},{1,0},{2,1},{3,2},{4,7},{5,4},{6,5},{7,6},{8,11},{9,8},{10,9... | collective-permute-start | bytes 177416 | tf_op jit(solution)/shard_map/ppermute | solution.py:29
  44.1 7.8 %collective-permute-start.9 = (bf16[64,2048]{1,0:T(8,128)(2,1)}, bf16[64,2048]{1,0:T(8,128)(2,1)}, u32[]{:S(2)}, u32[]{:S(2)}) collective-permute-start(bf16[64,2048]{1,0:T(8,128)(2,1)} %get-tuple-element.61), channel_id=1, source_target_pairs={{0,3},{1,0},{2,1},{3,2},{4,7},{5,4},{6,5},{7,6},{8,11},{9,8},{10,9... | collective-permute-start | bytes 786440 | tf_op jit(solution)/shard_map/ppermute | solution.py:29
  47.7 7.9 %collective-permute-start.10 = (bf16[64,2048]{1,0:T(8,128)(2,1)}, bf16[64,2048]{1,0:T(8,128)(2,1)}, u32[]{:S(2)}, u32[]{:S(2)}) collective-permute-start(bf16[64,2048]{1,0:T(8,128)(2,1)} %get-tuple-element.62), channel_id=1, source_target_pairs={{0,1},{1,2},{2,3},{3,0},{4,5},{5,6},{6,7},{7,4},{8,9},{9,10},{10,1... | collective-permute-start | bytes 786440 | tf_op jit(solution)/shard_map/ppermute | solution.py:29
  62.0 10.7 %collective-permute-start.11 = (bf16[4,64,462]{2,1,0:T(8,128)(2,1)S(1)}, bf16[4,64,462]{2,1,0:T(8,128)(2,1)S(1)}, u32[]{:S(2)}, u32[]{:S(2)}) collective-permute-start(bf16[4,64,462]{2,1,0:T(8,128)(2,1)S(1)} %get-tuple-element.69), channel_id=1, source_target_pairs={{0,8},{8,16},{16,24},{24,0},{1,9},{9,17},{17,25},{25,1},{2,10},{10... | collective-permute-start | bytes 709640 | tf_op jit(solution)/shard_map/ppermute | solution.py:29
  63.7 12.0 %collective-permute-start.12 = (bf16[4,64,462]{2,1,0:T(8,128)(2,1)S(1)}, bf16[4,64,462]{2,1,0:T(8,128)(2,1)S(1)}, u32[]{:S(2)}, u32[]{:S(2)}) collective-permute-start(bf16[4,64,462]{2,1,0:T(8,128)(2,1)S(1)} %get-tuple-element.70), channel_id=1, source_target_pairs={{0,16},{8,24},{16,0},{24,8},{1,17},{9,25},{17,1},{25,9},{2,18},{10... | collective-permute-start | bytes 709640 | tf_op jit(solution)/shard_map/ppermute | solution.py:29
  66.6 9.1 %collective-permute-start.13 = (bf16[4,64,462]{2,1,0:T(8,128)(2,1)S(1)}, bf16[4,64,462]{2,1,0:T(8,128)(2,1)S(1)}, u32[]{:S(2)}, u32[]{:S(2)}) collective-permute-start(bf16[4,64,462]{2,1,0:T(8,128)(2,1)S(1)} %get-tuple-element.71), channel_id=1, source_target_pairs={{0,24},{8,0},{16,8},{24,16},{1,25},{9,1},{17,9},{25,17},{2,26},{10... | collective-permute-start | bytes 709640 | tf_op jit(solution)/shard_map/ppermute | solution.py:29
  75.7 12.4 %collective-permute-start.14 = (bf16[4,64,462]{2,1,0:T(8,128)(2,1)S(1)}, bf16[4,64,462]{2,1,0:T(8,128)(2,1)S(1)}, u32[]{:S(2)}, u32[]{:S(2)}) collective-permute-start(bf16[4,64,462]{2,1,0:T(8,128)(2,1)S(1)} %get-tuple-element.82), channel_id=1, source_target_pairs={{0,8},{8,16},{16,24},{24,0},{1,9},{9,17},{17,25},{25,1},{2,10},{10... | collective-permute-start | bytes 709640 | tf_op jit(solution)/shard_map/ppermute | solution.py:29
  79.8 13.9 %collective-permute-start.15 = (bf16[4,64,462]{2,1,0:T(8,128)(2,1)S(1)}, bf16[4,64,462]{2,1,0:T(8,128)(2,1)S(1)}, u32[]{:S(2)}, u32[]{:S(2)}) collective-permute-start(bf16[4,64,462]{2,1,0:T(8,128)(2,1)S(1)} %get-tuple-element.83), channel_id=1, source_target_pairs={{0,16},{8,24},{16,0},{24,8},{1,17},{9,25},{17,1},{25,9},{2,18},{10... | collective-permute-start | bytes 709640 | tf_op jit(solution)/shard_map/ppermute | solution.py:29
  80.8 12.9 %collective-permute-start.16 = (bf16[4,64,462]{2,1,0:T(8,128)(2,1)S(1)}, bf16[4,64,462]{2,1,0:T(8,128)(2,1)S(1)}, u32[]{:S(2)}, u32[]{:S(2)}) collective-permute-start(bf16[4,64,462]{2,1,0:T(8,128)(2,1)S(1)} %get-tuple-element.84), channel_id=1, source_target_pairs={{0,24},{8,0},{16,8},{24,16},{1,25},{9,1},{17,9},{25,17},{2,26},{10... | collective-permute-start | bytes 709640 | tf_op jit(solution)/shard_map/ppermute | solution.py:29
  83.8 15.8 %collective-permute-start.19 = (bf16[4,64,462]{2,1,0:T(8,128)(2,1)S(1)}, bf16[4,64,462]{2,1,0:T(8,128)(2,1)S(1)}, u32[]{:S(2)}, u32[]{:S(2)}) collective-permute-start(bf16[4,64,462]{2,1,0:T(8,128)(2,1)S(1)} %gradient0.1.own), channel_id=1, source_target_pairs={{0,24},{8,0},{16,8},{24,16},{1,25},{9,1},{17,9},{25,17},{2,26},{10... | collective-permute-start | bytes 709640 | tf_op jit(solution)/shard_map/ppermute | solution.py:29
  85.3 16.0 %collective-permute-start.18 = (bf16[4,64,462]{2,1,0:T(8,128)(2,1)S(1)}, bf16[4,64,462]{2,1,0:T(8,128)(2,1)S(1)}, u32[]{:S(2)}, u32[]{:S(2)}) collective-permute-start(bf16[4,64,462]{2,1,0:T(8,128)(2,1)S(1)} %gradient0.1.own), channel_id=1, source_target_pairs={{0,16},{8,24},{16,0},{24,8},{1,17},{9,25},{17,1},{25,9},{2,18},{10... | collective-permute-start | bytes 709640 | tf_op jit(solution)/shard_map/ppermute | solution.py:29
  88.1 13.7 %collective-permute-start.17 = (bf16[4,64,462]{2,1,0:T(8,128)(2,1)S(1)}, bf16[4,64,462]{2,1,0:T(8,128)(2,1)S(1)}, u32[]{:S(2)}, u32[]{:S(2)}) collective-permute-start(bf16[4,64,462]{2,1,0:T(8,128)(2,1)S(1)} %gradient0.1.own), channel_id=1, source_target_pairs={{0,8},{8,16},{16,24},{24,0},{1,9},{9,17},{17,25},{25,1},{2,10},{10... | collective-permute-start | bytes 709640 | tf_op jit(solution)/shard_map/ppermute | solution.py:29
  95.0 15.8 %collective-permute-start.22 = (bf16[4,64,462]{2,1,0:T(8,128)(2,1)S(1)}, bf16[4,64,462]{2,1,0:T(8,128)(2,1)S(1)}, u32[]{:S(2)}, u32[]{:S(2)}) collective-permute-start(bf16[4,64,462]{2,1,0:T(8,128)(2,1)S(1)} %gradient1.1.own), channel_id=1, source_target_pairs={{0,24},{8,0},{16,8},{24,16},{1,25},{9,1},{17,9},{25,17},{2,26},{10... | collective-permute-start | bytes 709640 | tf_op jit(solution)/shard_map/ppermute | solution.py:29
  97.1 15.1 %collective-permute-start.21 = (bf16[4,64,462]{2,1,0:T(8,128)(2,1)S(1)}, bf16[4,64,462]{2,1,0:T(8,128)(2,1)S(1)}, u32[]{:S(2)}, u32[]{:S(2)}) collective-permute-start(bf16[4,64,462]{2,1,0:T(8,128)(2,1)S(1)} %gradient1.1.own), channel_id=1, source_target_pairs={{0,16},{8,24},{16,0},{24,8},{1,17},{9,25},{17,1},{25,9},{2,18},{10... | collective-permute-start | bytes 709640 | tf_op jit(solution)/shard_map/ppermute | solution.py:29
  99.6 12.7 %collective-permute-start.20 = (bf16[4,64,462]{2,1,0:T(8,128)(2,1)S(1)}, bf16[4,64,462]{2,1,0:T(8,128)(2,1)S(1)}, u32[]{:S(2)}, u32[]{:S(2)}) collective-permute-start(bf16[4,64,462]{2,1,0:T(8,128)(2,1)S(1)} %gradient1.1.own), channel_id=1, source_target_pairs={{0,8},{8,16},{16,24},{24,0},{1,9},{9,17},{17,25},{25,1},{2,10},{10... | collective-permute-start | bytes 709640 | tf_op jit(solution)/shard_map/ppermute | solution.py:29
  107.1 10.8 %collective-permute-start.23 = (bf16[64,2048]{1,0:T(8,128)(2,1)S(1)}, bf16[64,2048]{1,0:T(8,128)(2,1)S(1)}, u32[]{:S(2)}, u32[]{:S(2)}) collective-permute-start(bf16[64,2048]{1,0:T(8,128)(2,1)S(1)} %get-tuple-element.91), channel_id=1, source_target_pairs={{0,1},{1,2},{2,3},{3,0},{4,5},{5,6},{6,7},{7,4},{8,9},{9,10},{10,1... | collective-permute-start | bytes 786440 | tf_op jit(solution)/shard_map/ppermute | solution.py:29
  107.1 12.3 %collective-permute-start.24 = (bf16[64,2048]{1,0:T(8,128)(2,1)S(1)}, bf16[64,2048]{1,0:T(8,128)(2,1)S(1)}, u32[]{:S(2)}, u32[]{:S(2)}) collective-permute-start(bf16[64,2048]{1,0:T(8,128)(2,1)S(1)} %get-tuple-element.92), channel_id=1, source_target_pairs={{0,3},{1,0},{2,1},{3,2},{4,7},{5,4},{6,5},{7,6},{8,11},{9,8},{10,9... | collective-permute-start | bytes 786440 | tf_op jit(solution)/shard_map/ppermute | solution.py:29
  110.8 13.7 %collective-permute-start.25 = (bf16[64,2048]{1,0:T(8,128)(2,1)S(1)}, bf16[64,2048]{1,0:T(8,128)(2,1)S(1)}, u32[]{:S(2)}, u32[]{:S(2)}) collective-permute-start(bf16[64,2048]{1,0:T(8,128)(2,1)S(1)} %get-tuple-element.94), channel_id=1, source_target_pairs={{0,2},{1,3},{2,0},{3,1},{4,6},{5,7},{6,4},{7,5},{8,10},{9,11},{10,... | collective-permute-start | bytes 786440 | tf_op jit(solution)/shard_map/ppermute | solution.py:29
  117.2 22.6 %collective-permute-start.29 = (bf16[256,2048]{1,0:T(8,128)(2,1)}, bf16[256,2048]{1,0:T(8,128)(2,1)S(1)}, u32[]{:S(2)}, u32[]{:S(2)}) collective-permute-start(bf16[256,2048]{1,0:T(8,128)(2,1)} %get-tuple-element.102.refs_0_), channel_id=1, source_target_pairs={{0,32},{32,0},{1,33},{33,1},{2,34},{34,2},{3,35},{35,3},{4,36},{36... | collective-permute-start | bytes 3145736 | tf_op jit(solution)/shard_map/ppermute | solution.py:29
  117.2 22.6 %collective-permute-start.30 = (bf16[256,2048]{1,0:T(8,128)(2,1)}, bf16[256,2048]{1,0:T(8,128)(2,1)S(1)}, u32[]{:S(2)}, u32[]{:S(2)}) collective-permute-start(bf16[256,2048]{1,0:T(8,128)(2,1)} %get-tuple-element.103.refs_1_), channel_id=1, source_target_pairs={{0,32},{32,0},{1,33},{33,1},{2,34},{34,2},{3,35},{35,3},{4,36},{36... | collective-permute-start | bytes 3145736 | tf_op jit(solution)/shard_map/ppermute | solution.py:29
  119.4 13.6 %collective-permute-start.26 = (bf16[64,2048]{1,0:T(8,128)(2,1)S(1)}, bf16[64,2048]{1,0:T(8,128)(2,1)S(1)}, u32[]{:S(2)}, u32[]{:S(2)}) collective-permute-start(bf16[64,2048]{1,0:T(8,128)(2,1)S(1)} %get-tuple-element.97), channel_id=1, source_target_pairs={{0,1},{1,2},{2,3},{3,0},{4,5},{5,6},{6,7},{7,4},{8,9},{9,10},{10,1... | collective-permute-start | bytes 786440 | tf_op jit(solution)/shard_map/ppermute | solution.py:29
  119.4 13.6 %collective-permute-start.27 = (bf16[64,2048]{1,0:T(8,128)(2,1)S(1)}, bf16[64,2048]{1,0:T(8,128)(2,1)S(1)}, u32[]{:S(2)}, u32[]{:S(2)}) collective-permute-start(bf16[64,2048]{1,0:T(8,128)(2,1)S(1)} %get-tuple-element.98), channel_id=1, source_target_pairs={{0,2},{1,3},{2,0},{3,1},{4,6},{5,7},{6,4},{7,5},{8,10},{9,11},{10,... | collective-permute-start | bytes 786440 | tf_op jit(solution)/shard_map/ppermute | solution.py:29
  124.5 9.0 %collective-permute-start.28 = (bf16[64,2048]{1,0:T(8,128)(2,1)S(1)}, bf16[64,2048]{1,0:T(8,128)(2,1)S(1)}, u32[]{:S(2)}, u32[]{:S(2)}) collective-permute-start(bf16[64,2048]{1,0:T(8,128)(2,1)S(1)} %get-tuple-element.99), channel_id=1, source_target_pairs={{0,3},{1,0},{2,1},{3,2},{4,7},{5,4},{6,5},{7,6},{8,11},{9,8},{10,9... | collective-permute-start | bytes 786440 | tf_op jit(solution)/shard_map/ppermute | solution.py:29
  133.0 6.7 %collective-permute-start.31 = (bf16[2,4,64,462]{3,2,1,0:T(8,128)(2,1)S(1)}, bf16[2,4,64,462]{3,2,1,0:T(8,128)(2,1)}, u32[]{:S(2)}, u32[]{:S(2)}) collective-permute-start(bf16[2,4,64,462]{3,2,1,0:T(8,128)(2,1)S(1)} %get-tuple-element.106), channel_id=1, source_target_pairs={{0,32},{32,0},{1,33},{33,1},{2,34},{34,2},{3,35},{35,3},{4,36},{36... | collective-permute-start | bytes 1419272 | tf_op jit(solution)/shard_map/ppermute | solution.py:29
  134.5 21.4 %all-to-all-start.1 = ((bf16[8,16,2048]{2,1,0:T(8,128)(2,1)}), bf16[8,16,2048]{2,1,0:T(8,128)(2,1)S(1)}, u32[]{:S(2)}, u32[]{:S(2)}) async-start(bf16[8,16,2048]{2,1,0:T(8,128)(2,1)} %bitcast.28), calls=%async_computation.1 | async-start | bytes 1048576 | tf_op jit(solution)/shard_map/all_to_all | solution.py:45
  (11 other events, 97.5 us)

commit v2 on v1

--- a/solution.py
+++ b/solution.py
@@ -262,7 +262,7 @@
     tokens0, own0, *sent0 = forward(after(at, cot_sibling), 0, chunks[0], weights)
     got0 = [y_shift(t, s) for s, t in enumerate(sent0, 1)]
     tokens1, own1, *sent1 = forward(after(at, own0), 1, chunks[1], weights)
-    got0, sent1 = lax.optimization_barrier((got0, sent1))
+    got0[0], got0[2], sent1 = lax.optimization_barrier((got0[0], got0[2], sent1))
     got1 = [y_shift(t, s) for s, t in enumerate(sent1, 1)]
     grad0 = gradient(at, 0, own0, got0, cot, cot_sibling)
     pieces0 = [grad0] + [y_shift(grad0, s) for s in (1, 2, 3)]

time: 157 us -> 155 us (0.987)
  starting transfers between devices: 58.8 us -> 54.9 us
    ppermute x33, starting transfers between devices: 45 us -> 42.5 us  [shift(): lax.ppermute(value, axis, [(i, (i + by) % size) for i in range(size)])]
  transfers between devices with their start and end apart: 35 -> 35, of which waited for: 15 -> 16; matrix products, arithmetic and copies ran while one was open for 6% -> 6% of each run, Pallas kernels for 16% -> 16%
where the time goes in v2:
time: 155 us; the launch traced here: 154 us
  starting transfers between devices  54.9 us (35%)
  waiting for transfers between devices  53.3 us (34%)
  Pallas kernels  30.7 us (20%)
  local copies, waits for them, and re-layouts  11.5 us (7%)
  other arithmetic  2.9 us (2%)
    ppermute x33, starting transfers between devices, shift(): lax.ppermute(value, axis, [(i, (i + by) % size) for i in range(size)])  42.5 us
    ppermute x33, waiting for transfers between devices, shift(): lax.ppermute(value, axis, [(i, (i + by) % size) for i in range(size)])  35.1 us
    all_to_all x2, waiting for transfers between devices, exchange(): return lax.all_to_all(value, axes, split_axis=0, concat_axis=0, tiled=True)  18.1 us
    all_to_all x2, starting transfers between devices, exchange(): return lax.all_to_all(value, axes, split_axis=0, concat_axis=0, tiled=True)  12.4 us
    pallas_call x2, Pallas kernels, forward(): pl.pallas_call(functools.partial(forward_kernel, half), out_shape=(jax.Sh...  9.68 us
    pallas_call x2, Pallas kernels, backward(): pl.pallas_call(functools.partial(backward_kernel, min(512, width)), out_s...  9.42 us
    pallas_call x1, Pallas kernels, weight_grads(): pl.pallas_call(functools.partial(weights_kernel, min(512, width)), out_sh...  7.5 us
    unnamed x17, local copies, waits for them, and re-layouts  5.56 us
  transfers between devices with their start and end apart: 35, of which 16 were waited for; matrix products, arithmetic and copies ran while one was open for 6% of the time, Pallas kernels for 16%

profile of v2, /device:TPU:32, one launch (start us, length us, event | category | flops | bytes accessed | tf_op | source)
XLA Modules:
  0.0 154.2 jit_solution(13258109807636993809)
XLA Ops:
  1.2 1.7 %broadcast_in_dim.2 = bf16[8,16,2048]{2,1,0:T(8,128)(2,1)} broadcast(bf16[16,2048]{1,0:T(8,128)(2,1)} %param.4), dimensions={1,2} | broadcast | bytes 589824 | tf_op jit(solution)/shard_map/broadcast_in_dim | solution.py:248
  2.9 8.6 %all-to-all-start = ((bf16[8,16,2048]{2,1,0:T(8,128)(2,1)}), bf16[8,16,2048]{2,1,0:T(8,128)(2,1)S(1)}, u32[]{:S(2)}, u32[]{:S(2)}) async-start(bf16[8,16,2048]{2,1,0:T(8,128)(2,1)} %broadcast_in_dim.2), calls=%async_computation | async-start | bytes 1048576 | tf_op jit(solution)/shard_map/all_to_all | solution.py:45
  12.7 2.3 %reshape.21 = bf16[2,4,16,2,4,462]{5,4,3,2,1,0:T(4,128)(2,1)S(1)} reshape(bf16[128,3696]{1,0:T(8,128)(2,1)S(1)} %copy.8) | data formatting | bytes 1892352 | tf_op jit(solution)/shard_map/reshape | solution.py:244
  16.1 11.6 %all-to-all-done = bf16[8,16,2048]{2,1,0:T(8,128)(2,1)S(1)} async-done(((bf16[8,16,2048]{2,1,0:T(8,128)(2,1)}), bf16[8,16,2048]{2,1,0:T(8,128)(2,1)S(1)}, u32[]{:S(2)}, u32[]{:S(2)}) %all-to-all-start) | async-done | bytes 524320 | tf_op jit(solution)/shard_map/all_to_all | solution.py:45
  29.3 1.7 %collective-permute-start.7 = (bf16[128,2048]{1,0:T(8,128)(2,1)S(1)}, bf16[128,2048]{1,0:T(8,128)(2,1)S(1)}, u32[]{:S(2)}, u32[]{:S(2)}) collective-permute-start(bf16[128,2048]{1,0:T(8,128)(2,1)S(1)} %bitcast.25), channel_id=1, source_target_pairs={{0,3},{1,0},{2,1},{3,2},{4,7},{5,4},{6,5},{7,6},{8,11},{9,8},{10,9... | collective-permute-start | bytes 1572872 | tf_op jit(solution)/shard_map/ppermute | solution.py:29
  32.9 4.1 %collective-permute-done.2 = bf16[4,32,462]{2,1,0:T(8,128)(2,1)S(1)} collective-permute-done((bf16[4,32,462]{2,1,0:T(8,128)(2,1)S(1)}, bf16[4,32,462]{2,1,0:T(8,128)(2,1)S(1)}, u32[]{:S(2)}, u32[]{:S(2)}) %collective-permute-start.2) | collective-permute-done | bytes 118304 | tf_op jit(solution)/shard_map/ppermute | solution.py:29
  37.4 2.8 %collective-permute-start.4 = (bf16[2,32,462]{2,1,0:T(8,128)(2,1)S(1)}, bf16[2,32,462]{2,1,0:T(8,128)(2,1)S(1)}, u32[]{:S(2)}, u32[]{:S(2)}) collective-permute-start(bf16[2,32,462]{2,1,0:T(8,128)(2,1)S(1)} %pad_maximum_fusion.3), channel_id=1, source_target_pairs={{0,2},{1,3},{2,0},{3,1},{4,6},{5,7},{6,4},{7,5},{8,10},{9,11},{10,... | collective-permute-start | bytes 177416 | tf_op jit(solution)/shard_map/ppermute | solution.py:29
  40.2 1.5 collective-permute-start.5
  44.1 3.6 %collective-permute-start.9 = (bf16[64,2048]{1,0:T(8,128)(2,1)}, bf16[64,2048]{1,0:T(8,128)(2,1)}, u32[]{:S(2)}, u32[]{:S(2)}) collective-permute-start(bf16[64,2048]{1,0:T(8,128)(2,1)} %get-tuple-element.60), channel_id=1, source_target_pairs={{0,3},{1,0},{2,1},{3,2},{4,7},{5,4},{6,5},{7,6},{8,11},{9,8},{10,9... | collective-permute-start | bytes 786440 | tf_op jit(solution)/shard_map/ppermute | solution.py:29
  48.5 1.8 %collective-permute-done.6.cot_sibling = bf16[4,2,32,462]{3,2,1,0:T(8,128)(2,1)} collective-permute-done((bf16[4,2,32,462]{3,2,1,0:T(8,128)(2,1)}, bf16[4,2,32,462]{3,2,1,0:T(8,128)(2,1)}, u32[]{:S(2)}, u32[]{:S(2)}) %collective-permute-start.6) | collective-permute-done | bytes 236576 | tf_op jit(solution)/shard_map/ppermute | solution.py:29
  50.3 1.5 %collective-permute-done.9.refs_2_ = bf16[64,2048]{1,0:T(8,128)(2,1)} collective-permute-done((bf16[64,2048]{1,0:T(8,128)(2,1)}, bf16[64,2048]{1,0:T(8,128)(2,1)}, u32[]{:S(2)}, u32[]{:S(2)}) %collective-permute-start.9) | collective-permute-done | bytes 262176 | tf_op jit(solution)/shard_map/ppermute | solution.py:29
  51.9 3.7 %collective-permute-done.10.refs_2_ = bf16[64,2048]{1,0:T(8,128)(2,1)} collective-permute-done((bf16[64,2048]{1,0:T(8,128)(2,1)}, bf16[64,2048]{1,0:T(8,128)(2,1)}, u32[]{:S(2)}, u32[]{:S(2)}) %collective-permute-start.10) | collective-permute-done | bytes 262176 | tf_op jit(solution)/shard_map/ppermute | solution.py:29
  55.6 1.5 copy-done.1
  57.1 4.9 %forward0.1 = (bf16[256,2048]{1,0:T(8,128)(2,1)}, f32[4,64,462]{2,1,0:T(8,128)S(1)}, bf16[4,64,462]{2,1,0:T(8,128)(2,1)S(1)}, bf16[4,64,462]{2,1,0:T(8,128)(2,1)S(1)}, bf16[4,64,462]{2,1,0:T(8,128)(2,1)S(1)}) custom-call(s32[4]{0:T(128)S(1)} %pad_add_fusion.at_ref, bf16[128,2048]{1,0:T(8,128)(2,1)S(1)} %bitcast.26, ...), custom_call_target="tpu_custom_call" | custom-call | flops 110000000 | bytes 1 | tf_op jit(solution)/shard_map/forward0/pallas_call | solution.py:82
  62.0 1.6 %collective-permute-start.11 = (bf16[4,64,462]{2,1,0:T(8,128)(2,1)S(1)}, bf16[4,64,462]{2,1,0:T(8,128)(2,1)S(1)}, u32[]{:S(2)}, u32[]{:S(2)}) collective-permute-start(bf16[4,64,462]{2,1,0:T(8,128)(2,1)S(1)} %get-tuple-element.68), channel_id=1, source_target_pairs={{0,8},{8,16},{16,24},{24,0},{1,9},{9,17},{17,25},{25,1},{2,10},{10... | collective-permute-start | bytes 709640 | tf_op jit(solution)/shard_map/ppermute | solution.py:29
  63.7 1.7 %collective-permute-start.12 = (bf16[4,64,462]{2,1,0:T(8,128)(2,1)S(1)}, bf16[4,64,462]{2,1,0:T(8,128)(2,1)S(1)}, u32[]{:S(2)}, u32[]{:S(2)}) collective-permute-start(bf16[4,64,462]{2,1,0:T(8,128)(2,1)S(1)} %get-tuple-element.69), channel_id=1, source_target_pairs={{0,24},{8,0},{16,8},{24,16},{1,25},{9,1},{17,9},{25,17},{2,26},{10... | collective-permute-start | bytes 709640 | tf_op jit(solution)/shard_map/ppermute | solution.py:29
  65.3 2.0 %collective-permute-start.13 = (bf16[4,64,462]{2,1,0:T(8,128)(2,1)S(1)}, bf16[4,64,462]{2,1,0:T(8,128)(2,1)S(1)}, u32[]{:S(2)}, u32[]{:S(2)}) collective-permute-start(bf16[4,64,462]{2,1,0:T(8,128)(2,1)S(1)} %get-tuple-element.76), channel_id=1, source_target_pairs={{0,16},{8,24},{16,0},{24,8},{1,17},{9,25},{17,1},{25,9},{2,18},{10... | collective-permute-start | bytes 709640 | tf_op jit(solution)/shard_map/ppermute | solution.py:29
  67.3 4.8 %forward1.1 = (bf16[256,2048]{1,0:T(8,128)(2,1)}, f32[4,64,462]{2,1,0:T(8,128)S(1)}, bf16[4,64,462]{2,1,0:T(8,128)(2,1)S(1)}, bf16[4,64,462]{2,1,0:T(8,128)(2,1)S(1)}, bf16[4,64,462]{2,1,0:T(8,128)(2,1)S(1)}) custom-call(s32[4]{0:T(128)S(1)} %pad_add_fusion.at_ref, bf16[128,2048]{1,0:T(8,128)(2,1)S(1)} %bitcast.27, ...), custom_call_target="tpu_custom_call" | custom-call | flops 110000000 | bytes 1 | tf_op jit(solution)/shard_map/forward1/pallas_call | solution.py:82
  72.9 7.2 %collective-permute-start.15 = (bf16[4,64,462]{2,1,0:T(8,128)(2,1)S(1)}, bf16[4,64,462]{2,1,0:T(8,128)(2,1)S(1)}, u32[]{:S(2)}, u32[]{:S(2)}) collective-permute-start(bf16[4,64,462]{2,1,0:T(8,128)(2,1)S(1)} %get-tuple-element.81), channel_id=1, source_target_pairs={{0,16},{8,24},{16,0},{24,8},{1,17},{9,25},{17,1},{25,9},{2,18},{10... | collective-permute-start | bytes 709640 | tf_op jit(solution)/shard_map/ppermute | solution.py:29
  82.0 3.5 %collective-permute-start.18 = (bf16[4,64,462]{2,1,0:T(8,128)(2,1)S(1)}, bf16[4,64,462]{2,1,0:T(8,128)(2,1)S(1)}, u32[]{:S(2)}, u32[]{:S(2)}) collective-permute-start(bf16[4,64,462]{2,1,0:T(8,128)(2,1)S(1)} %gradient0.1.own), channel_id=1, source_target_pairs={{0,16},{8,24},{16,0},{24,8},{1,17},{9,25},{17,1},{25,9},{2,18},{10... | collective-permute-start | bytes 709640 | tf_op jit(solution)/shard_map/ppermute | solution.py:29
  85.5 2.8 %collective-permute-done.14.from1 = bf16[4,64,462]{2,1,0:T(8,128)(2,1)S(1)} collective-permute-done((bf16[4,64,462]{2,1,0:T(8,128)(2,1)S(1)}, bf16[4,64,462]{2,1,0:T(8,128)(2,1)S(1)}, u32[]{:S(2)}, u32[]{:S(2)}) %collective-permute-start.14) | collective-permute-done | bytes 236576 | tf_op jit(solution)/shard_map/ppermute | solution.py:29
  88.3 4.7 %collective-permute-done.15.from2 = bf16[4,64,462]{2,1,0:T(8,128)(2,1)S(1)} collective-permute-done((bf16[4,64,462]{2,1,0:T(8,128)(2,1)S(1)}, bf16[4,64,462]{2,1,0:T(8,128)(2,1)S(1)}, u32[]{:S(2)}, u32[]{:S(2)}) %collective-permute-start.15) | collective-permute-done | bytes 236576 | tf_op jit(solution)/shard_map/ppermute | solution.py:29
  94.3 2.5 %collective-permute-start.22 = (bf16[4,64,462]{2,1,0:T(8,128)(2,1)S(1)}, bf16[4,64,462]{2,1,0:T(8,128)(2,1)S(1)}, u32[]{:S(2)}, u32[]{:S(2)}) collective-permute-start(bf16[4,64,462]{2,1,0:T(8,128)(2,1)S(1)} %gradient1.1.own), channel_id=1, source_target_pairs={{0,24},{8,0},{16,8},{24,16},{1,25},{9,1},{17,9},{25,17},{2,26},{10... | collective-permute-start | bytes 709640 | tf_op jit(solution)/shard_map/ppermute | solution.py:29
  98.5 3.3 %collective-permute-done.17.from1 = bf16[4,64,462]{2,1,0:T(8,128)(2,1)S(1)} collective-permute-done((bf16[4,64,462]{2,1,0:T(8,128)(2,1)S(1)}, bf16[4,64,462]{2,1,0:T(8,128)(2,1)S(1)}, u32[]{:S(2)}, u32[]{:S(2)}) %collective-permute-start.17) | collective-permute-done | bytes 236576 | tf_op jit(solution)/shard_map/ppermute | solution.py:29
  101.8 4.5 %backward0.1 = (bf16[2,4,64,462]{3,2,1,0:T(8,128)(2,1)S(1)}, bf16[2,4,64,462]{3,2,1,0:T(8,128)(2,1)S(1)}, f32[64,2048]{1,0:T(8,128)S(1)}, bf16[64,2048]{1,0:T(8,...) custom-call(s32[4]{0:T(128)S(1)} %pad_add_fusion.at_ref, ...), custom_call_target="tpu_custom_call" | custom-call | flops 5500000256 | bytes 1 | tf_op jit(solution)/shard_map/backward0/pallas_call | solution.py:152
  107.1 3.2 %collective-permute-start.24 = (bf16[64,2048]{1,0:T(8,128)(2,1)S(1)}, bf16[64,2048]{1,0:T(8,128)(2,1)S(1)}, u32[]{:S(2)}, u32[]{:S(2)}) collective-permute-start(bf16[64,2048]{1,0:T(8,128)(2,1)S(1)} %get-tuple-element.90), channel_id=1, source_target_pairs={{0,3},{1,0},{2,1},{3,2},{4,7},{5,4},{6,5},{7,6},{8,11},{9,8},{10,9... | collective-permute-start | bytes 786440 | tf_op jit(solution)/shard_map/ppermute | solution.py:29
  111.4 4.9 %backward1.1 = (bf16[2,4,64,462]{3,2,1,0:T(8,128)(2,1)S(1)}, bf16[2,4,64,462]{3,2,1,0:T(8,128)(2,1)}, f32[64,2048]{1,0:T(8,128)S(1)}, bf16[64,2048]{1,0:T(8,128)...) custom-call(s32[4]{0:T(128)S(1)} %pad_add_fusion.at_ref, bf16[4,64,462]{2,1,0:T(8,128)(2,1)S(1)} %gradient1.1.own, ...), custom_call_target="tpu_custom_call" | custom-call | flops 5500000256 | bytes 1 | tf_op jit(solution)/shard_map/backward1/pallas_call | solution.py:152
  118.2 4.0 %collective-permute-start.27 = (bf16[64,2048]{1,0:T(8,128)(2,1)S(1)}, bf16[64,2048]{1,0:T(8,128)(2,1)S(1)}, u32[]{:S(2)}, u32[]{:S(2)}) collective-permute-start(bf16[64,2048]{1,0:T(8,128)(2,1)S(1)} %get-tuple-element.96), channel_id=1, source_target_pairs={{0,2},{1,3},{2,0},{3,1},{4,6},{5,7},{6,4},{7,5},{8,10},{9,11},{10,... | collective-permute-start | bytes 786440 | tf_op jit(solution)/shard_map/ppermute | solution.py:29
  122.4 9.6 %collective-permute-done.26 = bf16[64,2048]{1,0:T(8,128)(2,1)S(1)} collective-permute-done((bf16[64,2048]{1,0:T(8,128)(2,1)S(1)}, bf16[64,2048]{1,0:T(8,128)(2,1)S(1)}, u32[]{:S(2)}, u32[]{:S(2)}) %collective-permute-start.26) | collective-permute-done | bytes 262176 | tf_op jit(solution)/shard_map/ppermute | solution.py:29
  133.5 3.9 %all-to-all-start.1 = ((bf16[8,16,2048]{2,1,0:T(8,128)(2,1)}), bf16[8,16,2048]{2,1,0:T(8,128)(2,1)S(1)}, u32[]{:S(2)}, u32[]{:S(2)}) async-start(bf16[8,16,2048]{2,1,0:T(8,128)(2,1)} %bitcast.28), calls=%async_computation.1 | async-start | bytes 1048576 | tf_op jit(solution)/shard_map/all_to_all | solution.py:45
  139.5 7.5 %weight_grads.1 = (bf16[462,2048]{1,0:T(8,128)(2,1)}, bf16[462,2048]{1,0:T(8,128)(2,1)}) custom-call(bf16[256,2048]{1,0:T(8,128)(2,1)} %get-tuple-element.100.refs_0_, bf16[256,2048]{1,0:T(8,128)(2,1)} %get-tuple-element.101.refs_1_, bf16[256,2048]{1,0:T(8,128)(2,1)S(1)} %collective-permute-done.29.refs_2_, ...), custom_call_target="tpu_custom_call" | custom-call | flops 11000000512 | bytes 1 | tf_op jit(solution)/shard_map/weight_grads/pallas_call | solution.py:187
  147.0 6.5 %all-to-all-done.1.got = bf16[8,16,2048]{2,1,0:T(8,128)(2,1)S(1)} async-done(((bf16[8,16,2048]{2,1,0:T(8,128)(2,1)}), bf16[8,16,2048]{2,1,0:T(8,128)(2,1)S(1)}, u32[]{:S(2)}, u32[]{:S(2)}) %all-to-all-start.1) | async-done | bytes 524320 | tf_op jit(solution)/shard_map/all_to_all | solution.py:45
  (82 shorter events, 23.8 us)
Async XLA Ops:
  0.6 27.2 %collective-permute-start = (bf16[462,2048]{1,0:T(8,128)(2,1)}, bf16[462,2048]{1,0:T(8,128)(2,1)}, u32[]{:S(2)}, u32[]{:S(2)}) collective-permute-start(bf16[462,2048]{1,0:T(8,128)(2,1)} %refs_0_.1), channel_id=1, source_target_pairs={{0,32},{32,0},{1,33},{33,1},{2,34},{34,2},{3,35},{35,3},{4,36},{36... | collective-permute-start | bytes 5677064 | tf_op jit(solution)/shard_map/ppermute | solution.py:29
  0.7 27.1 %collective-permute-start.1 = (bf16[462,2048]{1,0:T(8,128)(2,1)}, bf16[462,2048]{1,0:T(8,128)(2,1)}, u32[]{:S(2)}, u32[]{:S(2)}) collective-permute-start(bf16[462,2048]{1,0:T(8,128)(2,1)} %refs_1_.1), channel_id=1, source_target_pairs={{0,32},{32,0},{1,33},{33,1},{2,34},{34,2},{3,35},{35,3},{4,36},{36... | collective-permute-start | bytes 5677064 | tf_op jit(solution)/shard_map/ppermute | solution.py:29
  2.9 24.9 %all-to-all-start = ((bf16[8,16,2048]{2,1,0:T(8,128)(2,1)}), bf16[8,16,2048]{2,1,0:T(8,128)(2,1)S(1)}, u32[]{:S(2)}, u32[]{:S(2)}) async-start(bf16[8,16,2048]{2,1,0:T(8,128)(2,1)} %broadcast_in_dim.2), calls=%async_computation | async-start | bytes 1048576 | tf_op jit(solution)/shard_map/all_to_all | solution.py:45
  27.8 15.1 %collective-permute-start.8 = (bf16[128,2048]{1,0:T(8,128)(2,1)S(1)}, bf16[128,2048]{1,0:T(8,128)(2,1)S(1)}, u32[]{:S(2)}, u32[]{:S(2)}) collective-permute-start(bf16[128,2048]{1,0:T(8,128)(2,1)S(1)} %bitcast.24), channel_id=1, source_target_pairs={{0,1},{1,2},{2,3},{3,0},{4,5},{5,6},{6,7},{7,4},{8,9},{9,10},{10,1... | collective-permute-start | bytes 1572872 | tf_op jit(solution)/shard_map/ppermute | solution.py:29
  29.3 13.9 %collective-permute-start.7 = (bf16[128,2048]{1,0:T(8,128)(2,1)S(1)}, bf16[128,2048]{1,0:T(8,128)(2,1)S(1)}, u32[]{:S(2)}, u32[]{:S(2)}) collective-permute-start(bf16[128,2048]{1,0:T(8,128)(2,1)S(1)} %bitcast.25), channel_id=1, source_target_pairs={{0,3},{1,0},{2,1},{3,2},{4,7},{5,4},{6,5},{7,6},{8,11},{9,8},{10,9... | collective-permute-start | bytes 1572872 | tf_op jit(solution)/shard_map/ppermute | solution.py:29
  37.0 10.6 %collective-permute-start.3 = (bf16[2,32,462]{2,1,0:T(8,128)(2,1)S(1)}, bf16[2,32,462]{2,1,0:T(8,128)(2,1)S(1)}, u32[]{:S(2)}, u32[]{:S(2)}) collective-permute-start(bf16[2,32,462]{2,1,0:T(8,128)(2,1)S(1)} %pad_maximum_fusion.2), channel_id=1, source_target_pairs={{0,1},{1,2},{2,3},{3,0},{4,5},{5,6},{6,7},{7,4},{8,9},{9,10},{10,1... | collective-permute-start | bytes 177416 | tf_op jit(solution)/shard_map/ppermute | solution.py:29
  37.4 10.3 %collective-permute-start.4 = (bf16[2,32,462]{2,1,0:T(8,128)(2,1)S(1)}, bf16[2,32,462]{2,1,0:T(8,128)(2,1)S(1)}, u32[]{:S(2)}, u32[]{:S(2)}) collective-permute-start(bf16[2,32,462]{2,1,0:T(8,128)(2,1)S(1)} %pad_maximum_fusion.3), channel_id=1, source_target_pairs={{0,2},{1,3},{2,0},{3,1},{4,6},{5,7},{6,4},{7,5},{8,10},{9,11},{10,... | collective-permute-start | bytes 177416 | tf_op jit(solution)/shard_map/ppermute | solution.py:29
  40.2 7.4 %collective-permute-start.5 = (bf16[2,32,462]{2,1,0:T(8,128)(2,1)S(1)}, bf16[2,32,462]{2,1,0:T(8,128)(2,1)S(1)}, u32[]{:S(2)}, u32[]{:S(2)}) collective-permute-start(bf16[2,32,462]{2,1,0:T(8,128)(2,1)S(1)} %pad_maximum_fusion.4), channel_id=1, source_target_pairs={{0,3},{1,0},{2,1},{3,2},{4,7},{5,4},{6,5},{7,6},{8,11},{9,8},{10,9... | collective-permute-start | bytes 177416 | tf_op jit(solution)/shard_map/ppermute | solution.py:29
  44.1 7.8 %collective-permute-start.9 = (bf16[64,2048]{1,0:T(8,128)(2,1)}, bf16[64,2048]{1,0:T(8,128)(2,1)}, u32[]{:S(2)}, u32[]{:S(2)}) collective-permute-start(bf16[64,2048]{1,0:T(8,128)(2,1)} %get-tuple-element.60), channel_id=1, source_target_pairs={{0,3},{1,0},{2,1},{3,2},{4,7},{5,4},{6,5},{7,6},{8,11},{9,8},{10,9... | collective-permute-start | bytes 786440 | tf_op jit(solution)/shard_map/ppermute | solution.py:29
  47.7 7.9 %collective-permute-start.10 = (bf16[64,2048]{1,0:T(8,128)(2,1)}, bf16[64,2048]{1,0:T(8,128)(2,1)}, u32[]{:S(2)}, u32[]{:S(2)}) collective-permute-start(bf16[64,2048]{1,0:T(8,128)(2,1)} %get-tuple-element.61), channel_id=1, source_target_pairs={{0,1},{1,2},{2,3},{3,0},{4,5},{5,6},{6,7},{7,4},{8,9},{9,10},{10,1... | collective-permute-start | bytes 786440 | tf_op jit(solution)/shard_map/ppermute | solution.py:29
  62.0 10.1 %collective-permute-start.11 = (bf16[4,64,462]{2,1,0:T(8,128)(2,1)S(1)}, bf16[4,64,462]{2,1,0:T(8,128)(2,1)S(1)}, u32[]{:S(2)}, u32[]{:S(2)}) collective-permute-start(bf16[4,64,462]{2,1,0:T(8,128)(2,1)S(1)} %get-tuple-element.68), channel_id=1, source_target_pairs={{0,8},{8,16},{16,24},{24,0},{1,9},{9,17},{17,25},{25,1},{2,10},{10... | collective-permute-start | bytes 709640 | tf_op jit(solution)/shard_map/ppermute | solution.py:29
  63.7 8.4 %collective-permute-start.12 = (bf16[4,64,462]{2,1,0:T(8,128)(2,1)S(1)}, bf16[4,64,462]{2,1,0:T(8,128)(2,1)S(1)}, u32[]{:S(2)}, u32[]{:S(2)}) collective-permute-start(bf16[4,64,462]{2,1,0:T(8,128)(2,1)S(1)} %get-tuple-element.69), channel_id=1, source_target_pairs={{0,24},{8,0},{16,8},{24,16},{1,25},{9,1},{17,9},{25,17},{2,26},{10... | collective-permute-start | bytes 709640 | tf_op jit(solution)/shard_map/ppermute | solution.py:29
  65.3 14.7 %collective-permute-start.13 = (bf16[4,64,462]{2,1,0:T(8,128)(2,1)S(1)}, bf16[4,64,462]{2,1,0:T(8,128)(2,1)S(1)}, u32[]{:S(2)}, u32[]{:S(2)}) collective-permute-start(bf16[4,64,462]{2,1,0:T(8,128)(2,1)S(1)} %get-tuple-element.76), channel_id=1, source_target_pairs={{0,16},{8,24},{16,0},{24,8},{1,17},{9,25},{17,1},{25,9},{2,18},{10... | collective-permute-start | bytes 709640 | tf_op jit(solution)/shard_map/ppermute | solution.py:29
  72.1 16.2 %collective-permute-start.14 = (bf16[4,64,462]{2,1,0:T(8,128)(2,1)S(1)}, bf16[4,64,462]{2,1,0:T(8,128)(2,1)S(1)}, u32[]{:S(2)}, u32[]{:S(2)}) collective-permute-start(bf16[4,64,462]{2,1,0:T(8,128)(2,1)S(1)} %get-tuple-element.80), channel_id=1, source_target_pairs={{0,8},{8,16},{16,24},{24,0},{1,9},{9,17},{17,25},{25,1},{2,10},{10... | collective-permute-start | bytes 709640 | tf_op jit(solution)/shard_map/ppermute | solution.py:29
  72.9 20.1 %collective-permute-start.15 = (bf16[4,64,462]{2,1,0:T(8,128)(2,1)S(1)}, bf16[4,64,462]{2,1,0:T(8,128)(2,1)S(1)}, u32[]{:S(2)}, u32[]{:S(2)}) collective-permute-start(bf16[4,64,462]{2,1,0:T(8,128)(2,1)S(1)} %get-tuple-element.81), channel_id=1, source_target_pairs={{0,16},{8,24},{16,0},{24,8},{1,17},{9,25},{17,1},{25,9},{2,18},{10... | collective-permute-start | bytes 709640 | tf_op jit(solution)/shard_map/ppermute | solution.py:29
  80.0 12.9 %collective-permute-start.16 = (bf16[4,64,462]{2,1,0:T(8,128)(2,1)S(1)}, bf16[4,64,462]{2,1,0:T(8,128)(2,1)S(1)}, u32[]{:S(2)}, u32[]{:S(2)}) collective-permute-start(bf16[4,64,462]{2,1,0:T(8,128)(2,1)S(1)} %get-tuple-element.82), channel_id=1, source_target_pairs={{0,24},{8,0},{16,8},{24,16},{1,25},{9,1},{17,9},{25,17},{2,26},{10... | collective-permute-start | bytes 709640 | tf_op jit(solution)/shard_map/ppermute | solution.py:29
  81.4 16.6 %collective-permute-start.19 = (bf16[4,64,462]{2,1,0:T(8,128)(2,1)S(1)}, bf16[4,64,462]{2,1,0:T(8,128)(2,1)S(1)}, u32[]{:S(2)}, u32[]{:S(2)}) collective-permute-start(bf16[4,64,462]{2,1,0:T(8,128)(2,1)S(1)} %gradient0.1.own), channel_id=1, source_target_pairs={{0,24},{8,0},{16,8},{24,16},{1,25},{9,1},{17,9},{25,17},{2,26},{10... | collective-permute-start | bytes 709640 | tf_op jit(solution)/shard_map/ppermute | solution.py:29
  82.0 16.5 %collective-permute-start.18 = (bf16[4,64,462]{2,1,0:T(8,128)(2,1)S(1)}, bf16[4,64,462]{2,1,0:T(8,128)(2,1)S(1)}, u32[]{:S(2)}, u32[]{:S(2)}) collective-permute-start(bf16[4,64,462]{2,1,0:T(8,128)(2,1)S(1)} %gradient0.1.own), channel_id=1, source_target_pairs={{0,16},{8,24},{16,0},{24,8},{1,17},{9,25},{17,1},{25,9},{2,18},{10... | collective-permute-start | bytes 709640 | tf_op jit(solution)/shard_map/ppermute | solution.py:29
  88.3 13.5 %collective-permute-start.17 = (bf16[4,64,462]{2,1,0:T(8,128)(2,1)S(1)}, bf16[4,64,462]{2,1,0:T(8,128)(2,1)S(1)}, u32[]{:S(2)}, u32[]{:S(2)}) collective-permute-start(bf16[4,64,462]{2,1,0:T(8,128)(2,1)S(1)} %gradient0.1.own), channel_id=1, source_target_pairs={{0,8},{8,16},{16,24},{24,0},{1,9},{9,17},{17,25},{25,1},{2,10},{10... | collective-permute-start | bytes 709640 | tf_op jit(solution)/shard_map/ppermute | solution.py:29
  94.3 16.1 %collective-permute-start.22 = (bf16[4,64,462]{2,1,0:T(8,128)(2,1)S(1)}, bf16[4,64,462]{2,1,0:T(8,128)(2,1)S(1)}, u32[]{:S(2)}, u32[]{:S(2)}) collective-permute-start(bf16[4,64,462]{2,1,0:T(8,128)(2,1)S(1)} %gradient1.1.own), channel_id=1, source_target_pairs={{0,24},{8,0},{16,8},{24,16},{1,25},{9,1},{17,9},{25,17},{2,26},{10... | collective-permute-start | bytes 709640 | tf_op jit(solution)/shard_map/ppermute | solution.py:29
  96.8 14.6 %collective-permute-start.21 = (bf16[4,64,462]{2,1,0:T(8,128)(2,1)S(1)}, bf16[4,64,462]{2,1,0:T(8,128)(2,1)S(1)}, u32[]{:S(2)}, u32[]{:S(2)}) collective-permute-start(bf16[4,64,462]{2,1,0:T(8,128)(2,1)S(1)} %gradient1.1.own), channel_id=1, source_target_pairs={{0,16},{8,24},{16,0},{24,8},{1,17},{9,25},{17,1},{25,9},{2,18},{10... | collective-permute-start | bytes 709640 | tf_op jit(solution)/shard_map/ppermute | solution.py:29
  97.9 13.5 %collective-permute-start.20 = (bf16[4,64,462]{2,1,0:T(8,128)(2,1)S(1)}, bf16[4,64,462]{2,1,0:T(8,128)(2,1)S(1)}, u32[]{:S(2)}, u32[]{:S(2)}) collective-permute-start(bf16[4,64,462]{2,1,0:T(8,128)(2,1)S(1)} %gradient1.1.own), channel_id=1, source_target_pairs={{0,8},{8,16},{16,24},{24,0},{1,9},{9,17},{17,25},{25,1},{2,10},{10... | collective-permute-start | bytes 709640 | tf_op jit(solution)/shard_map/ppermute | solution.py:29
  107.1 9.7 %collective-permute-start.23 = (bf16[64,2048]{1,0:T(8,128)(2,1)S(1)}, bf16[64,2048]{1,0:T(8,128)(2,1)S(1)}, u32[]{:S(2)}, u32[]{:S(2)}) collective-permute-start(bf16[64,2048]{1,0:T(8,128)(2,1)S(1)} %get-tuple-element.89), channel_id=1, source_target_pairs={{0,1},{1,2},{2,3},{3,0},{4,5},{5,6},{6,7},{7,4},{8,9},{9,10},{10,1... | collective-permute-start | bytes 786440 | tf_op jit(solution)/shard_map/ppermute | solution.py:29
  107.1 10.0 %collective-permute-start.24 = (bf16[64,2048]{1,0:T(8,128)(2,1)S(1)}, bf16[64,2048]{1,0:T(8,128)(2,1)S(1)}, u32[]{:S(2)}, u32[]{:S(2)}) collective-permute-start(bf16[64,2048]{1,0:T(8,128)(2,1)S(1)} %get-tuple-element.90), channel_id=1, source_target_pairs={{0,3},{1,0},{2,1},{3,2},{4,7},{5,4},{6,5},{7,6},{8,11},{9,8},{10,9... | collective-permute-start | bytes 786440 | tf_op jit(solution)/shard_map/ppermute | solution.py:29
  110.4 11.9 %collective-permute-start.25 = (bf16[64,2048]{1,0:T(8,128)(2,1)S(1)}, bf16[64,2048]{1,0:T(8,128)(2,1)S(1)}, u32[]{:S(2)}, u32[]{:S(2)}) collective-permute-start(bf16[64,2048]{1,0:T(8,128)(2,1)S(1)} %get-tuple-element.92), channel_id=1, source_target_pairs={{0,2},{1,3},{2,0},{3,1},{4,6},{5,7},{6,4},{7,5},{8,10},{9,11},{10,... | collective-permute-start | bytes 786440 | tf_op jit(solution)/shard_map/ppermute | solution.py:29
  116.3 21.1 %collective-permute-start.29 = (bf16[256,2048]{1,0:T(8,128)(2,1)}, bf16[256,2048]{1,0:T(8,128)(2,1)S(1)}, u32[]{:S(2)}, u32[]{:S(2)}) collective-permute-start(bf16[256,2048]{1,0:T(8,128)(2,1)} %get-tuple-element.100.refs_0_), channel_id=1, source_target_pairs={{0,32},{32,0},{1,33},{33,1},{2,34},{34,2},{3,35},{35,3},{4,36},{36... | collective-permute-start | bytes 3145736 | tf_op jit(solution)/shard_map/ppermute | solution.py:29
  116.3 21.1 %collective-permute-start.30 = (bf16[256,2048]{1,0:T(8,128)(2,1)}, bf16[256,2048]{1,0:T(8,128)(2,1)S(1)}, u32[]{:S(2)}, u32[]{:S(2)}) collective-permute-start(bf16[256,2048]{1,0:T(8,128)(2,1)} %get-tuple-element.101.refs_1_), channel_id=1, source_target_pairs={{0,32},{32,0},{1,33},{33,1},{2,34},{34,2},{3,35},{35,3},{4,36},{36... | collective-permute-start | bytes 3145736 | tf_op jit(solution)/shard_map/ppermute | solution.py:29
  117.1 14.8 %collective-permute-start.26 = (bf16[64,2048]{1,0:T(8,128)(2,1)S(1)}, bf16[64,2048]{1,0:T(8,128)(2,1)S(1)}, u32[]{:S(2)}, u32[]{:S(2)}) collective-permute-start(bf16[64,2048]{1,0:T(8,128)(2,1)S(1)} %get-tuple-element.95), channel_id=1, source_target_pairs={{0,1},{1,2},{2,3},{3,0},{4,5},{5,6},{6,7},{7,4},{8,9},{9,10},{10,1... | collective-permute-start | bytes 786440 | tf_op jit(solution)/shard_map/ppermute | solution.py:29
  118.2 13.7 %collective-permute-start.27 = (bf16[64,2048]{1,0:T(8,128)(2,1)S(1)}, bf16[64,2048]{1,0:T(8,128)(2,1)S(1)}, u32[]{:S(2)}, u32[]{:S(2)}) collective-permute-start(bf16[64,2048]{1,0:T(8,128)(2,1)S(1)} %get-tuple-element.96), channel_id=1, source_target_pairs={{0,2},{1,3},{2,0},{3,1},{4,6},{5,7},{6,4},{7,5},{8,10},{9,11},{10,... | collective-permute-start | bytes 786440 | tf_op jit(solution)/shard_map/ppermute | solution.py:29
  122.2 10.3 %collective-permute-start.28 = (bf16[64,2048]{1,0:T(8,128)(2,1)S(1)}, bf16[64,2048]{1,0:T(8,128)(2,1)S(1)}, u32[]{:S(2)}, u32[]{:S(2)}) collective-permute-start(bf16[64,2048]{1,0:T(8,128)(2,1)S(1)} %get-tuple-element.97), channel_id=1, source_target_pairs={{0,3},{1,0},{2,1},{3,2},{4,7},{5,4},{6,5},{7,6},{8,11},{9,8},{10,9... | collective-permute-start | bytes 786440 | tf_op jit(solution)/shard_map/ppermute | solution.py:29
  131.9 5.5 %collective-permute-start.31 = (bf16[2,4,64,462]{3,2,1,0:T(8,128)(2,1)S(1)}, bf16[2,4,64,462]{3,2,1,0:T(8,128)(2,1)}, u32[]{:S(2)}, u32[]{:S(2)}) collective-permute-start(bf16[2,4,64,462]{3,2,1,0:T(8,128)(2,1)S(1)} %get-tuple-element.104), channel_id=1, source_target_pairs={{0,32},{32,0},{1,33},{33,1},{2,34},{34,2},{3,35},{35,3},{4,36},{36... | collective-permute-start | bytes 1419272 | tf_op jit(solution)/shard_map/ppermute | solution.py:29
  133.5 20.0 %all-to-all-start.1 = ((bf16[8,16,2048]{2,1,0:T(8,128)(2,1)}), bf16[8,16,2048]{2,1,0:T(8,128)(2,1)S(1)}, u32[]{:S(2)}, u32[]{:S(2)}) async-start(bf16[8,16,2048]{2,1,0:T(8,128)(2,1)} %bitcast.28), calls=%async_computation.1 | async-start | bytes 1048576 | tf_op jit(solution)/shard_map/all_to_all | solution.py:45
  (11 other events, 95.5 us)
